TPU v7x, 512 devices: a whole 4x8x8 slice. The times are simulated.
512 devices in a mesh: ctx: 64 (over y, x, core), tp: 8 (over z).
Axes of the slice: x: 4, y: 8, z: 8, core: 2. Of those that a mesh axis runs over, the one named last changes fastest.
Arguments:
- query_act: bfloat16 [16384, 4096], P('ctx', 'tp'), may hold values from -6 to 6
- key_act: bfloat16 [16384, 4096], P('ctx', 'tp'), may hold values from -6 to 6
- value_act: bfloat16 [16384, 4096], P('ctx', 'tp'), may hold values from -6 to 6
- grad_gated: bfloat16 [16384, 4096], P('ctx', 'tp'), may hold values from -18 to 18
- filter_taps: float32 [128, 256], P('ctx', 'tp'), may hold values from -0.5 to 0.5
- decay_rate: float32 [256], P('tp'), may hold values from 0.002 to 0.03
Outputs:
- grad_query: bfloat16 [16384, 4096], P('ctx', 'tp')
- grad_key: bfloat16 [16384, 4096], P('ctx', 'tp')
- grad_value: bfloat16 [16384, 4096], P('ctx', 'tp')
- grad_filter: float32 [128, 256], P('ctx', 'tp')
All inputs are finite; a program needn't handle non-finite values.
Results may differ from a plain program's by a relative error of at most 0.001.
Values may be sent and summed in bfloat16 or wider, within the bound.
A program may use at most 64 MiB of HBM per device.

v0:
```python
import jax
import jax.numpy as jnp
from jax import lax
from jax.sharding import PartitionSpec as P

L = 128


highest = lax.Precision.HIGHEST


def passed_along(value, axis, steps):
    count = lax.axis_size(axis)
    first, last = (max(0, -steps), min(count, count - steps))
    return lax.ppermute(value, axis, [(source, source + steps) for source in range(first, last)])


def banded(vector_rows, width):
    groups = vector_rows.shape[0]
    tiled = jnp.tile(vector_rows, (1, width))
    tiled = tiled[:, : width * (3 * width - 1)].reshape(groups, width, 3 * width - 1)
    return tiled[:, :, : 2 * width]


def windows(extended, width, groups):
    length = extended.shape[0] - width
    lower = extended[:length].reshape(length // width, width, groups, -1)
    upper = extended[width:].reshape(length // width, width, groups, -1)
    return jnp.concatenate([lower, upper], axis=1)


def on_device(query_act, key_act, value_act, grad_gated, filter_taps, decay_rate):
    rows, channels = query_act.shape
    groups = decay_rate.shape[0]
    width = L
    per_group = channels // groups
    blocks = rows // width
    raw_full = lax.all_gather(filter_taps, "ctx", axis=0, tiled=True)
    tap_index = jnp.arange(width, dtype=jnp.float32)[:, None]
    damping = jnp.exp(-decay_rate[None, :] * tap_index)
    group_taps = (raw_full * damping).T
    causal_band = banded(
        jnp.concatenate(
            [
                jnp.zeros((groups, 1), jnp.float32),
                group_taps[:, ::-1],
                jnp.zeros((groups, 2 * width - 1), jnp.float32),
            ],
            axis=1,
        ),
        width,
    )
    anti_band = banded(
        jnp.concatenate([group_taps, jnp.zeros((groups, 2 * width), jnp.float32)], axis=1), width
    )
    before = passed_along(jnp.stack([key_act[rows - width :], value_act[rows - width :]]), "ctx", 1)
    after = passed_along(jnp.stack([grad_gated[:width], query_act[:width]]), "ctx", -1)
    products = key_act.astype(jnp.float32) * value_act.astype(jnp.float32)
    slopes = grad_gated.astype(jnp.float32) * query_act.astype(jnp.float32)
    earlier = before[0].astype(jnp.float32) * before[1].astype(jnp.float32)
    later = after[0].astype(jnp.float32) * after[1].astype(jnp.float32)
    gated_win = windows(jnp.concatenate([earlier, products], axis=0), width, groups)
    slope_win = windows(jnp.concatenate([slopes, later], axis=0), width, groups)
    mixed = jnp.einsum("gsm,bmgc->bsgc", causal_band, gated_win, precision=highest).reshape(
        rows, channels
    )
    back = jnp.einsum("gsm,bmgc->bsgc", anti_band, slope_win, precision=highest).reshape(
        rows, channels
    )
    grad_query = (grad_gated.astype(jnp.float32) * mixed).astype(jnp.bfloat16)
    grad_key = (back * value_act.astype(jnp.float32)).astype(jnp.bfloat16)
    grad_value = (back * key_act.astype(jnp.float32)).astype(jnp.bfloat16)
    slope_blocks = slopes.reshape(blocks, width, groups, per_group)
    correlation = jnp.einsum("bsgc,bmgc->gsm", slope_blocks, gated_win, precision=highest)
    flat = jnp.pad(correlation.reshape(groups, 2 * width * width), ((0, 0), (0, width)))
    skewed = flat.reshape(groups, width, 2 * width + 1)[:, :, 1 : width + 1]
    lagged = jnp.sum(skewed, axis=1)[:, ::-1]
    all_tokens = rows * lax.axis_size("ctx")
    partial_grad = lagged.T * damping / float(all_tokens)
    grad_filter = lax.psum_scatter(partial_grad, "ctx", scatter_dimension=0, tiled=True)
    return (grad_query, grad_key, grad_value, grad_filter)


def solution(mesh):
    return jax.shard_map(
        on_device,
        mesh=mesh,
        in_specs=(
            P("ctx", "tp"),
            P("ctx", "tp"),
            P("ctx", "tp"),
            P("ctx", "tp"),
            P("ctx", "tp"),
            P("tp"),
        ),
        out_specs=(P("ctx", "tp"), P("ctx", "tp"), P("ctx", "tp"), P("ctx", "tp")),
        check_vma=False,
    )
```

profile of v0, /device:TPU:1, one launch (start us, length us, event | category | flops | bytes accessed | tf_op | source)
XLA Modules:
  0.0 371.7 jit_solution(3023298109884041590)
XLA Ops:
  0.6 1.1 copy.52
  1.7 1.1 copy.61
  2.9 8.8 %collective-permute-start.1 = (bf16[2,128,512]{1,2,0:T(8,128)(2,1)S(1)}, bf16[2,128,512]{1,2,0:T(8,128)(2,1)S(1)}, u32[]{:S(2)}, u32[]{:S(2)}) collective-permute-start(bf16[2,128,512]{1,2,0:T(8,128)(2,1)S(1)} %pad_maximum_fusion.3), channel_id=1, source_target_pairs={{8,0},{16,8},{24,16},{32,24},{40,32},{48,40},{56,48},{64,56},{72,6... | collective-permute-start | bytes 786440 | tf_op jit(solution)/shard_map/ppermute | solution.py:15
  11.7 1.1 copy.53
  12.8 1.1 copy.54
  14.6 1.9 collective-permute-start
  17.2 37.6 %all-gather = f32[64,2,32]{2,1,0:T(2,128)S(1)} all-gather(f32[1,2,32]{2,1,0:T(2,128)} %bitcast.80), channel_id=1, replica_groups=mesh['ctx'=64,'tp'=8] {'ctx'}, dimensions={0}, use_global_device_ids=true | all-gather | bytes 16640 | tf_op jit(solution)/shard_map/all_gather | solution.py:38
  55.8 3.6 copy.77
  59.5 3.0 slice.70
  62.5 9.6 %reshape.61 = f32[32,128,383]{2,1,0:T(8,128)} reshape(f32[32,49024]{1,0:T(8,128)} %slice.70) | data formatting | bytes 12550144 | tf_op jit(solution)/shard_map/reshape | solution.py:21
  72.7 3.6 copy.75
  76.4 3.0 slice.64
  79.4 9.7 %reshape.57 = f32[32,128,383]{2,1,0:T(8,128)} reshape(f32[32,49024]{1,0:T(8,128)} %slice.64) | data formatting | bytes 12550144 | tf_op jit(solution)/shard_map/reshape | solution.py:21
  89.1 1.3 dynamic-slice
  91.4 6.1 %fusion.3 = f32[2,128,32,16]{1,3,0,2:T(8,128)S(1)} fusion(f32[32,128,383]{2,1,0:T(8,128)} %reshape.61, f32[2,128,32,16]{1,3,0,2:T(8,128)S(1)} %copy.65, f32[2,128,32,16]{1,3,0,2:T(8,128)S(1)} %copy.64), kind=kOutput, calls=%fused_computation.6 | convolution fusion | flops 402915328 | bytes 5767168 | tf_op jit(solution)/shard_map/gsm,bmgc->bsgc/dot_general | solution.py:67
  98.2 1.0 multiply_bitcast_fusion.1
  99.7 3.5 fusion.12
  103.2 2.4 copy.79
  105.7 2.2 pad.5
  107.9 7.9 %reshape.64 = f32[32,128,257]{2,1,0:T(8,128)} reshape(f32[32,32896]{1,0:T(8,128)} %pad.5) | data formatting | bytes 8421376 | tf_op jit(solution)/shard_map/reshape | solution.py:76
  115.8 2.8 slice_reduce_fusion
  118.9 243.5 %all-reduce.2 = f32[128,32]{1,0:T(8,128)S(1)} all-reduce(f32[128,32]{1,0:T(8,128)S(1)} %copy.68), channel_id=2, replica_groups=mesh['ctx'=64,'tp'=8] {'ctx'}, use_global_device_ids=true, to_apply=%region_1.2.clone | all-reduce | flops 4096 | bytes 32768
  362.4 5.9 %fusion.2 = f32[2,128,32,16]{1,3,0,2:T(8,128)S(1)} fusion(f32[2,256,32,16]{1,3,0,2:T(8,128)S(1)} %copy_dynamic-update-slice_fusion, f32[32,128,383]{2,1,0:T(8,128)} %reshape.57), kind=kOutput, calls=%fused_computation.5 | convolution fusion | flops 402653184 | bytes 5767168 | tf_op jit(solution)/shard_map/gsm,bmgc->bsgc/dot_general | solution.py:64
  368.6 0.8 copy.69
  (39 shorter events, 7.3 us)
Async XLA Ops:
  2.9 88.1 %collective-permute-start.1 = (bf16[2,128,512]{1,2,0:T(8,128)(2,1)S(1)}, bf16[2,128,512]{1,2,0:T(8,128)(2,1)S(1)}, u32[]{:S(2)}, u32[]{:S(2)}) collective-permute-start(bf16[2,128,512]{1,2,0:T(8,128)(2,1)S(1)} %pad_maximum_fusion.3), channel_id=1, source_target_pairs={{8,0},{16,8},{24,16},{32,24},{40,32},{48,40},{56,48},{64,56},{72,6... | collective-permute-start | bytes 786440 | tf_op jit(solution)/shard_map/ppermute | solution.py:15
  14.6 83.6 %collective-permute-start = (bf16[2,128,512]{1,2,0:T(8,128)(2,1)}, bf16[2,128,512]{1,2,0:T(8,128)(2,1)}, u32[]{:S(2)}, u32[]{:S(2)}) collective-permute-start(bf16[2,128,512]{1,2,0:T(8,128)(2,1)} %pad_maximum_fusion.2), channel_id=1, source_target_pairs={{0,8},{8,16},{16,24},{24,32},{32,40},{40,48},{48,56},{56,64},{64,7... | collective-permute-start | bytes 786440 | tf_op jit(solution)/shard_map/ppermute | solution.py:15
where the time goes:
time: 375 us; the launch traced here: 372 us
  blocking collectives  281 us (75%)
  local copies, waits for them, and re-layouts  57 us (15%)
  matrix products  15.5 us (4%)
  starting transfers between devices  10.7 us (3%)
  other arithmetic  5.8 us (2%)
    unnamed x1, blocking collectives  243 us
    all_gather x1, blocking collectives, on_device(): raw_full = lax.all_gather(filter_taps, 'ctx', axis=0, tiled=True)  37.6 us
    reshape x2, local copies, waits for them, and re-layouts, banded(): tiled[:, :width * (3 * width - 1)].reshape(groups, width, 3 * width - 1)  19.3 us
    unnamed x14, local copies, waits for them, and re-layouts  18.5 us
    ppermute x2, starting transfers between devices, passed_along(): lax.ppermute(value, axis, [(source, source + steps) for source in range(f...  10.7 us
    reshape x1, local copies, waits for them, and re-layouts, on_device(): skewed = flat.reshape(groups, width, 2 * width + 1)[:, :, 1:width + 1]  7.94 us
  transfers between devices with their start and end apart: 2, of which 0 were waited for; matrix products, arithmetic and copies ran while one was open for 12% of the time, Pallas kernels for 0%

commit v1 on v0

v1 whole, which is shorter than its diff:
```python
import functools

import jax
import jax.numpy as jnp
from jax import lax
from jax.experimental import pallas as pl
from jax.experimental.pallas import tpu as pltpu
from jax.sharding import PartitionSpec as P

L = 128
CH = 16
LANES = 128
CHUNKS = 4
GROUPS = LANES // CH
MESH = pl.DeviceIdType.MESH
F32, BF16 = jnp.float32, jnp.bfloat16


def dot(a, b, dims):
    return lax.dot_general(a, b, (dims, ((), ())), preferred_element_type=F32)


def split_product(a, b):
    whole = jnp.transpose(a.astype(F32) * b.astype(F32))
    high = whole.astype(BF16)
    return high, (whole - high.astype(F32)).astype(BF16)


def prepare(c, k, v, g, q, pt, st):
    for (a, b, out, first) in ((k, v, pt, L), (g, q, st, 0)):
        high, low = split_product(a[c], b[c])
        out[c, 0, :, first : first + 2 * L] = high
        out[c, 1, :, first : first + 2 * L] = low


def prepare_halo(c, halo, out, first, here):
    high, low = split_product(halo[c, 0], halo[c, 1])
    keep = jnp.where(here, 1.0, 0.0).astype(BF16)
    out[c, 0, :, first : first + L] = high * keep
    out[c, 1, :, first : first + L] = low * keep


def lag_inner(c, pt, st, diag):
    row = lax.broadcasted_iota(jnp.int32, (L, L), 0)
    lane = lax.broadcasted_iota(jnp.int32, (L, L), 1)
    upper = lane >= row
    none = jnp.zeros((CH, L), BF16)
    for r in range(GROUPS):
        rows = slice(CH * r, CH * r + CH)
        p = [[pt[c, part, rows, L * b : L * b + L] for b in (1, 2)] for part in (0, 1)]
        s = [[st[c, part, rows, L * b : L * b + L] for b in (0, 1)] for part in (0, 1)]
        left = jnp.concatenate([p[0][0], p[0][1], p[1][0], p[1][1], p[0][0], p[0][1]], axis=0)
        right = jnp.concatenate(
            [
                jnp.concatenate([s[part][0], s[part][1]], axis=1) if b == 0 else jnp.concatenate([s[part][1], none], axis=1)
                for part in (0, 0, 1)
                for b in (0, 1)
            ],
            axis=0,
        )
        both = dot(left, right, ((0,), (0,)))
        diag[c, r] = jnp.where(upper, both[:, :L], both[:, L:])


def lag_cross(c, pt, st, pb, sb, diag, folded, lag):
    row = lax.broadcasted_iota(jnp.int32, (L, L), 0)
    lane = lax.broadcasted_iota(jnp.int32, (L, L), 1)
    upper = lane >= row
    none = jnp.zeros((CH, L), BF16)
    for r in range(0, GROUPS, 2):
        left, right = [], []
        for e in range(2):
            rows = slice(CH * (r + e), CH * (r + e) + CH)
            p = [pt[c, part, rows, pl.ds(pl.multiple_of(pb * L, L), L)] for part in (0, 1)]
            s = [st[c, part, rows, pl.ds(pl.multiple_of(sb * L, L), L)] for part in (0, 1)]
            for i, j in ((0, 0), (1, 0), (0, 1)):
                left.append(p[i])
                right.append(jnp.concatenate([s[j], none] if e == 0 else [none, s[j]], axis=1))
        both = dot(jnp.concatenate(left, axis=0), jnp.concatenate(right, axis=0), ((0,), (0,)))
        for e in range(2):
            whole = diag[c, r + e] + jnp.where(upper, 0.0, both[:, L * e : L * e + L])
            total = whole[:8]
            for a in range(8, L, 8):
                total = total + pltpu.roll(whole[a : a + 8], L - a, 1)
            folded[8 * (r + e) : 8 * (r + e) + 8, :] = total
    total = folded[pl.ds(0, GROUPS, stride=8), :]
    for a in range(1, 8):
        total = total + pltpu.roll(folded[pl.ds(a, GROUPS, stride=8), :], L - a, 1)
    lag[c] = total


def toeplitz(c, taps, band):
    row = lax.broadcasted_iota(jnp.int32, (L, L), 0)
    lane = lax.broadcasted_iota(jnp.int32, (L, L), 1)
    upper = jnp.where(lane >= row, 1.0, 0.0).astype(BF16)
    for r in range(GROUPS):
        line = taps[c, r : r + 1, :]
        whole = pltpu.roll(jnp.broadcast_to(line, (L, L)), 0, 1, stride=1, stride_axis=0)
        high = whole.astype(BF16)
        low = (whole - high.astype(F32)).astype(BF16)
        for i, part in ((0, high), (1, low)):
            now = part * upper
            band[c, r, L:, L * i : L * i + L] = now
            band[c, r, :L, L * i : L * i + L] = part - now


def convolve(c, pt, st, band, mixed, back):
    for r in range(GROUPS):
        rows = slice(CH * r, CH * r + CH)
        w = band[c, r]
        w_back = jnp.concatenate(
            [
                jnp.concatenate([w[L:, :L], w[:L, :L]], axis=1),
                jnp.concatenate([w[L:, L:], w[:L, L:]], axis=1),
            ],
            axis=0,
        )
        for x, weights, dims, out in ((pt, w, ((1,), (0,)), mixed), (st, w_back, ((1,), (1,)), back)):
            left = jnp.concatenate(
                [x[c, part, rows, L * b : L * b + 2 * L] for part in (0, 1) for b in (0, 1)], axis=0
            )
            got = dot(left, weights, dims)
            for b in (0, 1):
                out[rows, L * b : L * b + L] = (
                    got[CH * b : CH * b + CH, :L]
                    + got[CH * b : CH * b + CH, L:]
                    + got[CH * (2 + b) : CH * (2 + b) + CH, :L]
                )


def finish(c, k, v, g, mixed, back, out):
    forward = jnp.transpose(mixed[...])
    backward = jnp.transpose(back[...])
    out[0, c] = (g[c].astype(F32) * forward).astype(BF16)
    out[1, c] = (backward * v[c].astype(F32)).astype(BF16)
    out[2, c] = (backward * k[c].astype(F32)).astype(BF16)


def kernel(
    ny, nx, rows_here,
    k_hbm, v_hbm, q_hbm, g_hbm, taps_in, decay_in,
    gq_hbm, gk_hbm, gv_hbm, gf_out,
    k, v, q, g, kv_halo, qg_halo, pt, st, band, diag, folded, taps, lag, mixed, back, out,
    mine, gather_x, gather_y, partial, reduce_y, reduce_mine, reduce_x, final, summed,
    in_sem, out_sem, kv_send, kv_recv, qg_send, qg_recv,
    gx_send, gx_recv, gy_send, gy_recv, ry_send, ry_recv, rx_send, rx_recv,
):
    n = ny * nx
    me = lax.axis_index("ctx")
    y, xc = me // nx, me % nx
    core = me % 2
    nxt, prv = (me + 1) % n, (me + n - 1) % n
    tokens = 2 * L

    def at_x(d):
        return y * nx + (xc + d) % nx

    def at_y(d):
        return ((y + d) % ny) * nx + xc

    def lanes(c):
        return pl.ds(pl.multiple_of(c * LANES, LANES), LANES)

    def loads(c):
        return [
            pltpu.make_async_copy(src.at[:, lanes(c)], dst.at[c], in_sem.at[i, c])
            for i, (src, dst) in enumerate(((k_hbm, k), (v_hbm, v), (g_hbm, g), (q_hbm, q)))
        ]

    def stores(c):
        return [
            pltpu.make_async_copy(out.at[i, c], dst.at[:, lanes(c)], out_sem.at[i, c])
            for i, dst in enumerate((gq_hbm, gk_hbm, gv_hbm))
        ]

    def kv_copies(c):
        return [
            pltpu.make_async_remote_copy(
                src_ref=src.at[tokens - L :, lanes(c)], dst_ref=kv_halo.at[c, i],
                send_sem=kv_send.at[c, i], recv_sem=kv_recv.at[c, i],
                device_id={"ctx": nxt}, device_id_type=MESH,
            )
            for i, src in enumerate((k_hbm, v_hbm))
        ]

    def qg_copies(c):
        return [
            pltpu.make_async_remote_copy(
                src_ref=src.at[:L, lanes(c)], dst_ref=qg_halo.at[c, i],
                send_sem=qg_send.at[c, i], recv_sem=qg_recv.at[c, i],
                device_id={"ctx": prv}, device_id_type=MESH,
            )
            for i, src in enumerate((g_hbm, q_hbm))
        ]

    def exchange(src, dst, slot, there, send, recv, d):
        return pltpu.make_async_remote_copy(
            src_ref=src, dst_ref=dst.at[slot], send_sem=send.at[d - 1], recv_sem=recv.at[d - 1],
            device_id={"ctx": there}, device_id_type=MESH,
        )

    def gx_copy(d):
        return exchange(mine, gather_x, xc, at_x(d), gx_send, gx_recv, d)

    def gy_copy(d):
        return exchange(reduce_mine, gather_y, y, at_y(d), gy_send, gy_recv, d)

    def ry_copy(d):
        return exchange(partial.at[(y + d) % ny], reduce_y, y, at_y(d), ry_send, ry_recv, d)

    def rx_copy(d):
        return exchange(final, reduce_x, xc, at_x(d), rx_send, rx_recv, d)

    def each(copy, count, act):
        def step(d, carry):
            act(copy(d))
            return carry

        lax.fori_loop(1, count, step, 0)

    for i in range(CHUNKS):
        for copy in loads(i):
            copy.start()

    barrier = pltpu.get_barrier_semaphore()

    def greet(there):
        pl.semaphore_signal(barrier, inc=1, device_id={"ctx": there}, device_id_type=MESH)

    greet(nxt)
    greet(prv)
    each(at_x, nx, greet)
    each(at_y, ny, greet)

    block = nx * rows_here
    row = lax.broadcasted_iota(jnp.int32, (block, L), 0)
    groups = taps_in.shape[1]
    whole = jnp.zeros((block, L), F32)
    for i in range(rows_here):
        line = jnp.concatenate([taps_in[i : i + 1, :], jnp.zeros((1, L - groups), F32)], axis=1)
        whole = jnp.where(row == xc * rows_here + i, line, whole)
    mine[...] = whole
    gather_x[pl.ds(xc, 1)] = whole[None]

    pl.semaphore_wait(barrier, 2 + (nx - 1) + (ny - 1))
    each(gx_copy, nx, lambda copy: copy.start())
    for i in range(CHUNKS):
        for copy in kv_copies(i):
            copy.start()
        for copy in qg_copies((i + 2) % CHUNKS):
            copy.start()

    def prepare_step(c, carry):
        for copy in loads(c):
            copy.wait()
        prepare(c, k, v, g, q, pt, st)
        lag_inner(c, pt, st, diag)
        return carry

    lax.fori_loop(0, 2, prepare_step, 0)
    each(gx_copy, nx, lambda copy: copy.wait_recv())
    total = gather_x[0]
    for i in range(1, nx):
        total = total + gather_x[i]
    reduce_mine[...] = total
    gather_y[pl.ds(y, 1)] = total[None]
    each(gy_copy, ny, lambda copy: copy.start())
    lax.fori_loop(2, CHUNKS, prepare_step, 0)

    each(gy_copy, ny, lambda copy: copy.wait_recv())
    decay = decay_in[...]
    decay = jnp.concatenate([decay, jnp.zeros((1, L - groups), F32)], axis=1)
    step = lax.broadcasted_iota(jnp.int32, (L, L), 0).astype(F32)
    all_taps = gather_y[...].reshape(L, L) * jnp.exp(-decay * step)
    turned = jnp.transpose(all_taps)
    for c in range(CHUNKS):
        taps[c] = turned[GROUPS * c : GROUPS * c + GROUPS]

    def toeplitz_step(c, carry):
        toeplitz(c, taps, band)
        return carry

    lax.fori_loop(0, CHUNKS, toeplitz_step, 0)

    def kv_step(c, carry):
        for copy in kv_copies(c):
            copy.wait_recv()
        prepare_halo(c, kv_halo, pt, 0, me > 0)
        return carry

    def qg_step(c, carry):
        for copy in qg_copies(c):
            copy.wait_recv()
        prepare_halo(c, qg_halo, st, 2 * L, me < n - 1)
        return carry

    def cross_step(i, carry):
        c = (i + 2 - 2 * core) % CHUNKS

        @pl.when(c < 2)
        def _():
            kv_step(c, 0)

        @pl.when(c >= 2)
        def _():
            qg_step(c, 0)

        late = c // 2
        lag_cross(c, pt, st, 2 * late, 2 * late, diag, folded, lag)
        return carry

    lax.fori_loop(0, CHUNKS, cross_step, 0)

    per_lag = jnp.transpose(
        jnp.concatenate([lag[c] for c in range(CHUNKS)] + [jnp.zeros((L - CHUNKS * GROUPS, L), F32)], axis=0)
    )
    partial[...] = per_lag.reshape(ny, block, L)
    reduce_y[pl.ds(y, 1)] = partial[pl.ds(y, 1)]
    each(ry_copy, ny, lambda copy: copy.start())

    def output_step(i, carry):
        c = (i + 2 * core) % CHUNKS

        @pl.when(c < 2)
        def _():
            qg_step(c, 0)

        @pl.when(c >= 2)
        def _():
            kv_step(c, 0)

        convolve(c, pt, st, band, mixed, back)
        finish(c, k, v, g, mixed, back, out)
        for copy in stores(c):
            copy.start()
        return carry

    lax.fori_loop(0, 2, output_step, 0)
    each(ry_copy, ny, lambda copy: copy.wait_recv())
    total = reduce_y[0]
    for i in range(1, ny):
        total = total + reduce_y[i]
    final[...] = total
    reduce_x[pl.ds(xc, 1)] = total[None]
    each(rx_copy, nx, lambda copy: copy.start())
    lax.fori_loop(2, CHUNKS, output_step, 0)

    each(rx_copy, nx, lambda copy: copy.wait_recv())
    total = reduce_x[0]
    for i in range(1, nx):
        total = total + reduce_x[i]
    summed[...] = total
    lag_index = (me * rows_here + lax.broadcasted_iota(jnp.int32, (rows_here, L), 0)).astype(F32)
    share = summed[pl.ds(xc * rows_here, rows_here), :] * jnp.exp(-decay * lag_index) / float(tokens * n)
    gf_out[...] = share[:, :groups]

    for i in range(CHUNKS):
        for copy in stores(i):
            copy.wait()
        for copy in kv_copies(i):
            copy.wait_send()
        for copy in qg_copies(i):
            copy.wait_send()
    each(gx_copy, nx, lambda copy: copy.wait_send())
    each(gy_copy, ny, lambda copy: copy.wait_send())
    each(ry_copy, ny, lambda copy: copy.wait_send())
    each(rx_copy, nx, lambda copy: copy.wait_send())


def on_device(ny, nx, query_act, key_act, value_act, grad_gated, filter_taps, decay_rate):
    tokens, channels = query_act.shape
    rows_here, groups = filter_taps.shape
    block = nx * rows_here
    whole = jax.ShapeDtypeStruct((tokens, channels), BF16)
    vmem = pl.BlockSpec(memory_space=pltpu.VMEM)
    hbm = pl.BlockSpec(memory_space=pl.ANY)
    dma = pltpu.SemaphoreType.DMA
    chunked = pltpu.VMEM((CHUNKS, tokens, LANES), BF16)
    halo = pltpu.VMEM((CHUNKS, 2, L, LANES), BF16)
    wide = pltpu.VMEM((CHUNKS, 2, LANES, 3 * L), BF16)
    return pl.pallas_call(
        functools.partial(kernel, ny, nx, rows_here),
        out_shape=(whole, whole, whole, jax.ShapeDtypeStruct((rows_here, groups), F32)),
        in_specs=[hbm] * 4 + [vmem] * 2,
        out_specs=(hbm, hbm, hbm, vmem),
        scratch_shapes=[
            chunked, chunked, chunked, chunked, halo, halo, wide, wide,
            pltpu.VMEM((CHUNKS, GROUPS, 2 * L, 2 * L), BF16),
            pltpu.VMEM((CHUNKS, GROUPS, L, L), F32),
            pltpu.VMEM((8 * GROUPS, L), F32),
            pltpu.VMEM((CHUNKS, GROUPS, L), F32),
            pltpu.VMEM((CHUNKS, GROUPS, L), F32),
            pltpu.VMEM((LANES, tokens), F32),
            pltpu.VMEM((LANES, tokens), F32),
            pltpu.VMEM((3, CHUNKS, tokens, LANES), BF16),
            pltpu.VMEM((block, L), F32),
            pltpu.VMEM((nx, block, L), F32),
            pltpu.VMEM((ny, block, L), F32),
            pltpu.VMEM((ny, block, L), F32),
            pltpu.VMEM((ny, block, L), F32),
            pltpu.VMEM((block, L), F32),
            pltpu.VMEM((nx, block, L), F32),
            pltpu.VMEM((block, L), F32),
            pltpu.VMEM((block, L), F32),
            dma((4, CHUNKS)), dma((3, CHUNKS)),
            dma((CHUNKS, 2)), dma((CHUNKS, 2)), dma((CHUNKS, 2)), dma((CHUNKS, 2)),
            dma((nx - 1,)), dma((nx - 1,)), dma((ny - 1,)), dma((ny - 1,)),
            dma((ny - 1,)), dma((ny - 1,)), dma((nx - 1,)), dma((nx - 1,)),
        ],
        compiler_params=pltpu.CompilerParams(
            collective_id=0, has_side_effects=True, vmem_limit_bytes=60 * 1024 * 1024
        ),
    )(key_act, value_act, query_act, grad_gated, filter_taps, decay_rate.reshape(1, groups))


def solution(mesh):
    n = mesh.shape["ctx"]
    nx = 8 if n >= 64 else 4
    return jax.shard_map(
        functools.partial(on_device, n // nx, nx),
        mesh=mesh,
        in_specs=(P("ctx", "tp"),) * 5 + (P("tp"),),
        out_specs=(P("ctx", "tp"),) * 4,
        check_vma=False,
    )
```

time: 375 us -> 36.8 us (0.10)
  blocking collectives: 281 us -> 0 us
  local copies, waits for them, and re-layouts: 57 us -> 4.03 us
  Pallas kernels: 0 us -> 31.9 us
  matrix products: 15.5 us -> 0 us
  starting transfers between devices: 10.7 us -> 0 us
  other arithmetic: 5.8 us -> 0 us
    unnamed x1 -> x0, blocking collectives: 243 us -> none
    all_gather x1 -> x0, blocking collectives: 37.6 us -> none  [on_device(): raw_full = lax.all_gather(filter_taps, 'ctx', axis=0, tiled=True)]
    pallas_call x0 -> x1, Pallas kernels: none -> 31.9 us  [on_device(): pl.pallas_call(functools.partial(kernel, ny, nx, rows_here), out_shape=(w...]
    reshape x9 -> x0, local copies, waits for them, and re-layouts: 28.4 us -> none  [the longest x2 19.3 us: banded(): tiled[:, :width * (3 * width - 1)].reshape(groups, width, 3 * width - 1)]
    dot_general x3 -> x0, matrix products: 15.5 us -> none  [the longest x1 6.13 us: on_device(): jnp.einsum('gsm,bmgc->bsgc', anti_band, slope_win, precision=highest)]
    unnamed x14 -> x10, local copies, waits for them, and re-layouts: 18.5 us -> 4.03 us
    ppermute x2 -> x0, starting transfers between devices: 10.7 us -> none  [passed_along(): lax.ppermute(value, axis, [(source, source + steps) for source in range(f...]
    slice x2 -> x0, local copies, waits for them, and re-layouts: 6.05 us -> none  [banded(): tiled[:, :width * (3 * width - 1)].reshape(groups, width, 3 * width - 1)]
  transfers between devices with their start and end apart: 2 -> 0, of which waited for: 0 -> 0; matrix products, arithmetic and copies ran while one was open for 12% -> 0% of each run, Pallas kernels for 0% -> 0%
where the time goes in v1:
time: 36.8 us; the launch traced here: 36.5 us
  Pallas kernels  31.9 us (87%)
  local copies, waits for them, and re-layouts  4.03 us (11%)
  between operations  0.65 us (2%)
    pallas_call x1, Pallas kernels, on_device(): pl.pallas_call(functools.partial(kernel, ny, nx, rows_here), out_shape=(w...  31.9 us
    unnamed x10, local copies, waits for them, and re-layouts  4.03 us

profile of v1, /device:TPU:1, one launch (start us, length us, event | category | flops | bytes accessed | tf_op | source)
XLA Modules:
  0.0 36.5 jit_solution(12466688915506489196)
XLA Ops:
  0.6 31.9 %shard_map.93 = (bf16[256,512]{1,0:T(8,128)(2,1)}, bf16[256,512]{1,0:T(8,128)(2,1)}, bf16[256,512]{1,0:T(8,128)(2,1)}, f32[2,32]{1,0:T(2,128)}) custom-call(bf16[256,512]{1,0:T(8,128)(2,1)} %k_hbm.1, bf16[256,512]{1,0:T(8,128)(2,1)} %v_hbm.1, bf16[256,512]{1,0:T(8,128)(2,1)} %q_hbm.1, bf16[256,512]{1,0:T(8,128)(2,1)} %g_hbm.1, f32[2,32]{1,0:T(2,128)} %taps_in.1, ...), custom_call_target="tpu_custom_call" | custom-call | tf_op jit(solution)/shard_map/pallas_call | solution.py:381
  32.5 0.0 copy-start.1
  32.5 1.7 %copy.14 = bf16[256,512]{1,0:T(8,128)(2,1)} copy(bf16[256,512]{1,0:T(8,128)(2,1)} %get-tuple-element.8) | data formatting | bytes 524288
  34.2 0.0 copy-done.1
  34.2 0.0 copy-start
  34.2 0.7 %copy.15 = bf16[256,512]{1,0:T(8,128)(2,1)} copy(bf16[256,512]{1,0:T(8,128)(2,1)S(1)} %copy-done.1) | data formatting | bytes 524288
  34.9 0.3 copy-done
  35.3 0.0 copy-start.2
  35.3 0.7 %copy.16 = bf16[256,512]{1,0:T(8,128)(2,1)} copy(bf16[256,512]{1,0:T(8,128)(2,1)S(1)} %copy-done) | data formatting | bytes 524288
  36.0 0.0 copy-done.2
  36.0 0.6 %copy.17 = f32[2,32]{1,0:T(2,128)} copy(f32[2,32]{1,0:T(2,128)S(1)} %copy-done.2) | data formatting | bytes 512
Async XLA Ops:
  32.5 1.7 %copy-start.1 = (bf16[256,512]{1,0:T(8,128)(2,1)S(1)}, bf16[256,512]{1,0:T(8,128)(2,1)}, u32[]{:S(2)}) copy-start(bf16[256,512]{1,0:T(8,128)(2,1)} %get-tuple-element.9) | copy-start | bytes 786436
  34.2 1.0 %copy-start = (bf16[256,512]{1,0:T(8,128)(2,1)S(1)}, bf16[256,512]{1,0:T(8,128)(2,1)}, u32[]{:S(2)}) copy-start(bf16[256,512]{1,0:T(8,128)(2,1)} %get-tuple-element.10) | copy-start | bytes 786436
  35.3 0.7 %copy-start.2 = (f32[2,32]{1,0:T(2,128)S(1)}, f32[2,32]{1,0:T(2,128)}, u32[]{:S(2)}) copy-start(f32[2,32]{1,0:T(2,128)} %get-tuple-element.11) | copy-start | bytes 772

commit v2 on v1

v2 whole, which is shorter than its diff:
```python
import functools

import jax
import jax.numpy as jnp
from jax import lax
from jax.experimental import pallas as pl
from jax.experimental.pallas import tpu as pltpu
from jax.sharding import PartitionSpec as P

L = 128
CH = 16
LANES = 128
CHUNKS = 4
GROUPS = LANES // CH
VMEM_LIMIT = 53 * 1024 * 1024
MESH = pl.DeviceIdType.MESH
F32, BF16 = jnp.float32, jnp.bfloat16


def dot(a, b, dims):
    return lax.dot_general(a, b, (dims, ((), ())), preferred_element_type=F32)


def split_product(a, b):
    whole = jnp.transpose(a.astype(F32) * b.astype(F32))
    high = whole.astype(BF16)
    return high, (whole - high.astype(F32)).astype(BF16)


def lanes(c):
    return pl.ds(pl.multiple_of(c * LANES, LANES), LANES)


def prepare(c, k, v, g, q, pt, st):
    for (a, b, out, first) in ((k, v, pt, L), (g, q, st, 0)):
        high, low = split_product(a[:, lanes(c)], b[:, lanes(c)])
        out[c, 0, :, first : first + 2 * L] = high
        out[c, 1, :, first : first + 2 * L] = low


def prepare_halo(c, halo, out, first, here):
    high, low = split_product(halo[0, :, lanes(c)], halo[1, :, lanes(c)])
    keep = jnp.where(here, 1.0, 0.0).astype(BF16)
    out[c, 0, :, first : first + L] = high * keep
    out[c, 1, :, first : first + L] = low * keep


def lag_inner(c, pt, st, diag):
    row = lax.broadcasted_iota(jnp.int32, (L, L), 0)
    lane = lax.broadcasted_iota(jnp.int32, (L, L), 1)
    upper = lane >= row
    none = jnp.zeros((CH, L), BF16)
    for r in range(GROUPS):
        rows = slice(CH * r, CH * r + CH)
        p = [[pt[c, part, rows, L * b : L * b + L] for b in (1, 2)] for part in (0, 1)]
        s = [[st[c, part, rows, L * b : L * b + L] for b in (0, 1)] for part in (0, 1)]
        left = jnp.concatenate([p[0][0], p[0][1], p[1][0], p[1][1], p[0][0], p[0][1]], axis=0)
        right = jnp.concatenate(
            [
                jnp.concatenate([s[part][0], s[part][1]], axis=1) if b == 0 else jnp.concatenate([s[part][1], none], axis=1)
                for part in (0, 0, 1)
                for b in (0, 1)
            ],
            axis=0,
        )
        both = dot(left, right, ((0,), (0,)))
        diag[c, r] = jnp.where(upper, both[:, :L], both[:, L:])


def lag_cross(c, pt, st, pb, sb, diag, folded, lag):
    row = lax.broadcasted_iota(jnp.int32, (L, L), 0)
    lane = lax.broadcasted_iota(jnp.int32, (L, L), 1)
    upper = lane >= row
    none = jnp.zeros((CH, L), BF16)
    for r in range(0, GROUPS, 2):
        left, right = [], []
        for e in range(2):
            rows = slice(CH * (r + e), CH * (r + e) + CH)
            p = [pt[c, part, rows, pl.ds(pl.multiple_of(pb * L, L), L)] for part in (0, 1)]
            s = [st[c, part, rows, pl.ds(pl.multiple_of(sb * L, L), L)] for part in (0, 1)]
            for i, j in ((0, 0), (1, 0), (0, 1)):
                left.append(p[i])
                right.append(jnp.concatenate([s[j], none] if e == 0 else [none, s[j]], axis=1))
        both = dot(jnp.concatenate(left, axis=0), jnp.concatenate(right, axis=0), ((0,), (0,)))
        for e in range(2):
            whole = diag[c, r + e] + jnp.where(upper, 0.0, both[:, L * e : L * e + L])
            total = whole[:8]
            for a in range(8, L, 8):
                total = total + pltpu.roll(whole[a : a + 8], L - a, 1)
            folded[8 * (r + e) : 8 * (r + e) + 8, :] = total
    total = folded[pl.ds(0, GROUPS, stride=8), :]
    for a in range(1, 8):
        total = total + pltpu.roll(folded[pl.ds(a, GROUPS, stride=8), :], L - a, 1)
    lag[c] = total


def toeplitz(c, taps, band):
    row = lax.broadcasted_iota(jnp.int32, (L, L), 0)
    lane = lax.broadcasted_iota(jnp.int32, (L, L), 1)
    upper = jnp.where(lane >= row, 1.0, 0.0).astype(BF16)
    for r in range(GROUPS):
        line = taps[c, r : r + 1, :]
        whole = pltpu.roll(jnp.broadcast_to(line, (L, L)), 0, 1, stride=1, stride_axis=0)
        high = whole.astype(BF16)
        low = (whole - high.astype(F32)).astype(BF16)
        for i, part in ((0, high), (1, low)):
            now = part * upper
            band[c, r, L:, L * i : L * i + L] = now
            band[c, r, :L, L * i : L * i + L] = part - now


def convolve(c, pt, st, band, mixed, back):
    for r in range(GROUPS):
        rows = slice(CH * r, CH * r + CH)
        w = band[c, r]
        w_back = jnp.concatenate(
            [
                jnp.concatenate([w[L:, :L], w[:L, :L]], axis=1),
                jnp.concatenate([w[L:, L:], w[:L, L:]], axis=1),
            ],
            axis=0,
        )
        for x, weights, dims, out in ((pt, w, ((1,), (0,)), mixed), (st, w_back, ((1,), (1,)), back)):
            left = jnp.concatenate(
                [x[c, part, rows, L * b : L * b + 2 * L] for part in (0, 1) for b in (0, 1)], axis=0
            )
            got = dot(left, weights, dims)
            for b in (0, 1):
                out[rows, L * b : L * b + L] = (
                    got[CH * b : CH * b + CH, :L]
                    + got[CH * b : CH * b + CH, L:]
                    + got[CH * (2 + b) : CH * (2 + b) + CH, :L]
                )


def finish(c, k, v, g, mixed, back, gq, gk, gv):
    forward = jnp.transpose(mixed[...])
    backward = jnp.transpose(back[...])
    gq[:, lanes(c)] = (g[:, lanes(c)].astype(F32) * forward).astype(BF16)
    gk[:, lanes(c)] = (backward * v[:, lanes(c)].astype(F32)).astype(BF16)
    gv[:, lanes(c)] = (backward * k[:, lanes(c)].astype(F32)).astype(BF16)


def kernel(
    ny, nx, rows_here,
    k_hbm, v_hbm, q_hbm, g_hbm, taps_in, decay_in,
    gq, gk, gv, gf,
    k, v, q, g, kv_halo, qg_halo, pt, st, band, diag, folded, taps, lag, mixed, back,
    mine, gather_x, column, gather_y, partial, reduce_y, final, reduce_x, summed,
    in_sem, kv_send, kv_recv, qg_send, qg_recv, send, recv,
):
    n = ny * nx
    me = lax.axis_index("ctx")
    y, xc = me // nx, me % nx
    core = me % 2
    nxt, prv = (me + 1) % n, (me + n - 1) % n
    tokens = 2 * L
    half = CHUNKS * LANES // 2
    block = nx * rows_here
    groups = taps_in.shape[1]

    at_x = [y * nx + (xc + d) % nx for d in range(1, nx)]
    at_y = [((y + d) % ny) * nx + xc for d in range(1, ny)]

    loads = [
        pltpu.make_async_copy(src, dst, in_sem.at[i])
        for i, (src, dst) in enumerate(((k_hbm, k), (v_hbm, v), (g_hbm, g), (q_hbm, q)))
    ]

    def halo_copies(h, sources, first, dst, sends, recvs, there):
        columns = pl.ds(pl.multiple_of(h * half, LANES), half)
        return [
            pltpu.make_async_remote_copy(
                src_ref=src.at[first : first + L, columns], dst_ref=dst.at[i, :, columns],
                send_sem=sends.at[h, i], recv_sem=recvs.at[h, i],
                device_id={"ctx": there}, device_id_type=MESH,
            )
            for i, src in enumerate(sources)
        ]

    def kv_copies(h):
        return halo_copies(h, (k_hbm, v_hbm), tokens - L, kv_halo, kv_send, kv_recv, nxt)

    def qg_copies(h):
        return halo_copies(h, (g_hbm, q_hbm), 0, qg_halo, qg_send, qg_recv, prv)

    def exchange(which, sources, dst, slot, there):
        for src, device in zip(sources, there):
            pltpu.make_async_remote_copy(
                src_ref=src, dst_ref=dst.at[slot], send_sem=send.at[which], recv_sem=recv.at[which],
                device_id={"ctx": device}, device_id_type=MESH,
            ).start()

    def all_of(which, dst, count):
        return pltpu.make_async_remote_copy(
            src_ref=dst.at[:count], dst_ref=dst.at[:count], send_sem=send.at[which], recv_sem=recv.at[which],
            device_id={"ctx": nxt}, device_id_type=MESH,
        )

    def add_up(slots):
        total = slots[0]
        for i in range(1, slots.shape[0]):
            total = total + slots[i]
        return total

    for copy in loads:
        copy.start()

    barrier = pltpu.get_barrier_semaphore()
    for there in [nxt, prv] + at_x + at_y:
        pl.semaphore_signal(barrier, inc=1, device_id={"ctx": there}, device_id_type=MESH)

    row = lax.broadcasted_iota(jnp.int32, (block, L), 0)
    whole = jnp.zeros((block, L), F32)
    for i in range(rows_here):
        line = jnp.concatenate([taps_in[i : i + 1, :], jnp.zeros((1, L - groups), F32)], axis=1)
        whole = jnp.where(row == xc * rows_here + i, line, whole)
    mine[...] = whole
    gather_x[pl.ds(xc, 1)] = whole[None]

    pl.semaphore_wait(barrier, 2 + (nx - 1) + (ny - 1))
    exchange(0, [mine] * (nx - 1), gather_x, xc, at_x)
    for h in range(2):
        for copy in kv_copies(h) + qg_copies(1 - h):
            copy.start()

    for copy in loads:
        copy.wait()

    def prepare_step(c, carry):
        prepare(c, k, v, g, q, pt, st)
        return carry

    lax.fori_loop(0, CHUNKS, prepare_step, 0)

    def inner_step(c, carry):
        lag_inner(c, pt, st, diag)
        return carry

    lax.fori_loop(0, CHUNKS, inner_step, 0)

    all_of(0, gather_x, nx - 1).wait_recv()
    total = add_up(gather_x)
    column[...] = total
    gather_y[pl.ds(y, 1)] = total[None]
    exchange(1, [column] * (ny - 1), gather_y, y, at_y)

    def kv_arrived(h):
        for copy in kv_copies(h):
            copy.wait_recv()

        def step(i, carry):
            prepare_halo(2 * h + i, kv_halo, pt, 0, me > 0)
            return carry

        lax.fori_loop(0, 2, step, 0)

    def qg_arrived(h):
        for copy in qg_copies(h):
            copy.wait_recv()

        def step(i, carry):
            prepare_halo(2 * h + i, qg_halo, st, 2 * L, me < n - 1)
            return carry

        lax.fori_loop(0, 2, step, 0)

    def cross_step(i, carry):
        h = (i + 1 - core) % 2

        @pl.when(h == 0)
        def _():
            kv_arrived(0)

        @pl.when(h == 1)
        def _():
            qg_arrived(1)

        def step(j, carry):
            lag_cross(2 * h + j, pt, st, 2 * h, 2 * h, diag, folded, lag)
            return carry

        lax.fori_loop(0, 2, step, 0)
        return carry

    lax.fori_loop(0, 2, cross_step, 0)

    per_lag = jnp.transpose(
        jnp.concatenate([lag[c] for c in range(CHUNKS)] + [jnp.zeros((L - CHUNKS * GROUPS, L), F32)], axis=0)
    )
    partial[...] = per_lag.reshape(ny, block, L)
    reduce_y[pl.ds(y, 1)] = partial[pl.ds(y, 1)]
    exchange(2, [partial.at[(y + d) % ny] for d in range(1, ny)], reduce_y, y, at_y)

    all_of(1, gather_y, ny - 1).wait_recv()
    decay = jnp.concatenate([decay_in[...], jnp.zeros((1, L - groups), F32)], axis=1)
    step = lax.broadcasted_iota(jnp.int32, (L, L), 0).astype(F32)
    turned = jnp.transpose(gather_y[...].reshape(L, L) * jnp.exp(-decay * step))
    for c in range(CHUNKS):
        taps[c] = turned[GROUPS * c : GROUPS * c + GROUPS]

    def output_step(c, carry):
        toeplitz(c, taps, band)
        convolve(c, pt, st, band, mixed, back)
        finish(c, k, v, g, mixed, back, gq, gk, gv)
        return carry

    def output_half(i):
        h = (i + core) % 2

        @pl.when(h == 0)
        def _():
            qg_arrived(0)

        @pl.when(h == 1)
        def _():
            kv_arrived(1)

        lax.fori_loop(2 * h, 2 * h + 2, output_step, 0)

    output_half(0)
    all_of(2, reduce_y, ny - 1).wait_recv()
    total = add_up(reduce_y)
    final[...] = total
    reduce_x[pl.ds(xc, 1)] = total[None]
    exchange(3, [final] * (nx - 1), reduce_x, xc, at_x)
    output_half(1)

    all_of(3, reduce_x, nx - 1).wait_recv()
    summed[...] = add_up(reduce_x)
    lag_index = (me * rows_here + lax.broadcasted_iota(jnp.int32, (rows_here, L), 0)).astype(F32)
    share = summed[pl.ds(xc * rows_here, rows_here), :] * jnp.exp(-decay * lag_index) / float(tokens * n)
    gf[...] = share[:, :groups]

    for h in range(2):
        for copy in kv_copies(h) + qg_copies(h):
            copy.wait_send()
    all_of(0, gather_x, nx - 1).wait_send()
    all_of(1, gather_y, ny - 1).wait_send()
    all_of(2, reduce_y, ny - 1).wait_send()
    all_of(3, reduce_x, nx - 1).wait_send()


def write_out(*refs):
    count = len(refs) // 2
    sems = refs[-1]
    copies = [pltpu.make_async_copy(refs[i], refs[count + i], sems.at[i]) for i in range(count)]
    for copy in copies:
        copy.start()
    for copy in copies:
        copy.wait()


def on_device(ny, nx, query_act, key_act, value_act, grad_gated, filter_taps, decay_rate):
    tokens, channels = query_act.shape
    rows_here, groups = filter_taps.shape
    block = nx * rows_here
    whole = jax.ShapeDtypeStruct((tokens, channels), BF16)
    shapes = (whole, whole, whole, jax.ShapeDtypeStruct((rows_here, groups), F32))
    vmem = pl.BlockSpec(memory_space=pltpu.VMEM)
    hbm = pl.BlockSpec(memory_space=pl.ANY)
    dma = pltpu.SemaphoreType.DMA
    inner = pltpu.VMEM((tokens, channels), BF16)
    halo = pltpu.VMEM((2, L, channels), BF16)
    wide = pltpu.VMEM((CHUNKS, 2, LANES, 3 * L), BF16)
    rows = pltpu.VMEM((block, L), F32)
    by_x, by_y = pltpu.VMEM((nx, block, L), F32), pltpu.VMEM((ny, block, L), F32)
    results = pl.pallas_call(
        functools.partial(kernel, ny, nx, rows_here),
        out_shape=shapes,
        in_specs=[hbm] * 4 + [vmem] * 2,
        out_specs=(vmem,) * 4,
        scratch_shapes=[
            inner, inner, inner, inner, halo, halo, wide, wide,
            pltpu.VMEM((CHUNKS, GROUPS, 2 * L, 2 * L), BF16),
            pltpu.VMEM((CHUNKS, GROUPS, L, L), F32),
            pltpu.VMEM((8 * GROUPS, L), F32),
            pltpu.VMEM((CHUNKS, GROUPS, L), F32),
            pltpu.VMEM((CHUNKS, GROUPS, L), F32),
            pltpu.VMEM((LANES, tokens), F32),
            pltpu.VMEM((LANES, tokens), F32),
            rows, by_x, rows, by_y, by_y, by_y, rows, by_x, rows,
            dma((4,)), dma((2, 2)), dma((2, 2)), dma((2, 2)), dma((2, 2)), dma((4,)), dma((4,)),
        ],
        compiler_params=pltpu.CompilerParams(
            collective_id=0, has_side_effects=True, vmem_limit_bytes=VMEM_LIMIT
        ),
    )(key_act, value_act, query_act, grad_gated, filter_taps, decay_rate.reshape(1, groups))
    return pl.pallas_call(
        write_out,
        out_shape=shapes,
        in_specs=[vmem] * 4,
        out_specs=(hbm,) * 4,
        scratch_shapes=[dma((4,))],
        compiler_params=pltpu.CompilerParams(vmem_limit_bytes=4 * 1024 * 1024),
    )(*results)


def solution(mesh):
    n = mesh.shape["ctx"]
    nx = 8 if n >= 64 else 4
    return jax.shard_map(
        functools.partial(on_device, n // nx, nx),
        mesh=mesh,
        in_specs=(P("ctx", "tp"),) * 5 + (P("tp"),),
        out_specs=(P("ctx", "tp"),) * 4,
        check_vma=False,
    )
```

time: 36.8 us -> 28 us (0.76)
  Pallas kernels: 31.9 us -> 26.5 us
  local copies, waits for them, and re-layouts: 4.03 us -> 0.68 us
    pallas_call x1 -> x2, Pallas kernels: 31.9 us -> 26.5 us  [the longest x1 25.6 us: on_device(): pl.pallas_call(functools.partial(kernel, ny, nx, rows_here), out_shape=sh...]
    unnamed x10 -> x4, local copies, waits for them, and re-layouts: 4.03 us -> 0.68 us
where the time goes in v2:
time: 28 us; the launch traced here: 27.8 us
  Pallas kernels  26.5 us (95%)
  local copies, waits for them, and re-layouts  0.68 us (2%)
  between operations  0.66 us (2%)
    pallas_call x1, Pallas kernels, on_device(): pl.pallas_call(functools.partial(kernel, ny, nx, rows_here), out_shape=sh...  25.6 us
    pallas_call x1, Pallas kernels, on_device(): pl.pallas_call(write_out, out_shape=shapes, in_specs=[vmem] * 4, out_spec...  0.91 us
    unnamed x4, local copies, waits for them, and re-layouts  0.68 us

profile of v2, /device:TPU:1, one launch (start us, length us, event | category | flops | bytes accessed | tf_op | source)
XLA Modules:
  0.0 27.8 jit_solution(11390624567105988035)
XLA Ops:
  0.6 0.0 copy-start.1
  0.6 0.0 copy-start
  0.7 0.6 %copy-done.1 = f32[32]{0:T(128)S(1)} copy-done((f32[32]{0:T(128)S(1)}, f32[32]{0:T(128)}, u32[]{:S(2)}) %copy-start.1) | copy-done | bytes 152
  1.3 0.0 copy-done
  1.3 25.6 %shard_map.93 = (bf16[256,512]{1,0:T(8,128)(2,1)S(1)}, bf16[256,512]{1,0:T(8,128)(2,1)S(1)}, bf16[256,512]{1,0:T(8,128)(2,1)S(1)}, f32[2,32]{1,0:T(2,128)S(1)}) custom-call(bf16[256,512]{1,0:T(8,128)(2,1)} %k_hbm.1, bf16[256,512]{1,0:T(8,128)(2,1)} %v_hbm.1, bf16[256,512]{1,0:T(8,128)(2,1)} %q_hbm.1, bf16[256,512]{1,0:T(8,128)(2,1)} %g_hbm.1, ...), custom_call_target="tpu_custom_call" | custom-call | tf_op jit(solution)/shard_map/pallas_call | solution.py:368
  26.9 0.9 %shard_map.94 = (bf16[256,512]{1,0:T(8,128)(2,1)}, bf16[256,512]{1,0:T(8,128)(2,1)}, bf16[256,512]{1,0:T(8,128)(2,1)}, f32[2,32]{1,0:T(2,128)}) custom-call(bf16[256,512]{1,0:T(8,128)(2,1)S(1)} %get-tuple-element.8.refs_0_, bf16[256,512]{1,0:T(8,128)(2,1)S(1)} %get-tuple-element.9.refs_1_, bf16[256,512]{1,0:T(8,128)(2,1)S(1)} %get-tuple-element.10.refs_2_, ...), custom_call_target="tpu_custom_call" | custom-call | tf_op jit(solution)/shard_map/pallas_call | solution.py:389
Async XLA Ops:
  0.6 0.7 %copy-start.1 = (f32[32]{0:T(128)S(1)}, f32[32]{0:T(128)}, u32[]{:S(2)}) copy-start(f32[32]{0:T(128)} %param.11) | copy-start | bytes 388
  0.6 0.7 %copy-start = (f32[2,32]{1,0:T(2,128)S(1)}, f32[2,32]{1,0:T(2,128)}, u32[]{:S(2)}) copy-start(f32[2,32]{1,0:T(2,128)} %taps_in.1) | copy-start | bytes 772

commit v3 on v2

v3 whole, which is shorter than its diff:
```python
import functools

import jax
import jax.numpy as jnp
from jax import lax
from jax.experimental import pallas as pl
from jax.experimental.pallas import tpu as pltpu
from jax.sharding import PartitionSpec as P

L = 128
CH = 16
LANES = 128
CHUNKS = 4
GROUPS = LANES // CH
VMEM_LIMIT = 53 * 1024 * 1024
MESH = pl.DeviceIdType.MESH
F32, BF16 = jnp.float32, jnp.bfloat16


def dot(a, b, dims):
    return lax.dot_general(a, b, (dims, ((), ())), preferred_element_type=F32)


def flip(x):
    turn = 7 - lax.broadcasted_iota(jnp.int32, (8, LANES), 0)
    tiles = [jnp.take_along_axis(x[i : i + 8], turn, axis=0) for i in range(0, x.shape[0], 8)]
    return jnp.concatenate(tiles[::-1], axis=0)


def split_product(a, b, backward):
    whole = a.astype(F32) * b.astype(F32)
    whole = jnp.transpose(flip(whole) if backward else whole)
    high = whole.astype(BF16)
    return high, (whole - high.astype(F32)).astype(BF16)


def lanes(c):
    return pl.ds(pl.multiple_of(c * LANES, LANES), LANES)


def prepare(c, k, v, g, q, pt, st):
    for (a, b, out, backward) in ((k, v, pt, False), (g, q, st, True)):
        high, low = split_product(a[:, lanes(c)], b[:, lanes(c)], backward)
        out[c, 0, :, L:] = high
        out[c, 1, :, L:] = low


def prepare_halo(c, halo, out, backward, here):
    high, low = split_product(halo[0, :, lanes(c)], halo[1, :, lanes(c)], backward)
    keep = jnp.where(here, 1.0, 0.0).astype(BF16)
    out[c, 0, :, :L] = high * keep
    out[c, 1, :, :L] = low * keep


def lag_inner(c, pt, st, diag):
    row = lax.broadcasted_iota(jnp.int32, (L, L), 0)
    lane = lax.broadcasted_iota(jnp.int32, (L, L), 1)
    upper = lane + row < L
    none = jnp.zeros((CH, L), BF16)
    for r in range(GROUPS):
        rows = slice(CH * r, CH * r + CH)
        p = [[pt[c, part, rows, L * b : L * b + L] for b in (1, 2)] for part in (0, 1)]
        s = [[st[c, part, rows, L * b : L * b + L] for b in (2, 1)] for part in (0, 1)]
        left = jnp.concatenate([p[0][0], p[0][1], p[1][0], p[1][1], p[0][0], p[0][1]], axis=0)
        right = jnp.concatenate(
            [
                jnp.concatenate([s[part][0], s[part][1]], axis=1) if b == 0 else jnp.concatenate([s[part][1], none], axis=1)
                for part in (0, 0, 1)
                for b in (0, 1)
            ],
            axis=0,
        )
        both = dot(left, right, ((0,), (0,)))
        diag[c, r] = jnp.where(upper, both[:, :L], both[:, L:])


def lag_cross(c, pt, st, pb, sb, diag, folded, lag):
    row = lax.broadcasted_iota(jnp.int32, (L, L), 0)
    lane = lax.broadcasted_iota(jnp.int32, (L, L), 1)
    upper = lane + row < L
    none = jnp.zeros((CH, L), BF16)
    for r in range(0, GROUPS, 2):
        left, right = [], []
        for e in range(2):
            rows = slice(CH * (r + e), CH * (r + e) + CH)
            p = [pt[c, part, rows, pl.ds(pl.multiple_of(pb * L, L), L)] for part in (0, 1)]
            s = [st[c, part, rows, pl.ds(pl.multiple_of(sb * L, L), L)] for part in (0, 1)]
            for i, j in ((0, 0), (1, 0), (0, 1)):
                left.append(p[i])
                right.append(jnp.concatenate([s[j], none] if e == 0 else [none, s[j]], axis=1))
        both = dot(jnp.concatenate(left, axis=0), jnp.concatenate(right, axis=0), ((0,), (0,)))
        for e in range(2):
            whole = diag[c, r + e] + jnp.where(upper, 0.0, both[:, L * e : L * e + L])
            total = whole[:8]
            for a in range(8, L, 8):
                total = total + pltpu.roll(whole[a : a + 8], a, 1)
            folded[8 * (r + e) : 8 * (r + e) + 8, :] = total
    total = folded[pl.ds(0, GROUPS, stride=8), :]
    for a in range(1, 8):
        total = total + pltpu.roll(folded[pl.ds(a, GROUPS, stride=8), :], a, 1)
    lag[c] = total


def toeplitz(c, taps, band):
    row = lax.broadcasted_iota(jnp.int32, (L, L), 0)
    lane = lax.broadcasted_iota(jnp.int32, (L, L), 1)
    upper = jnp.where(lane >= row, 1.0, 0.0).astype(BF16)
    for r in range(GROUPS):
        line = taps[c, r : r + 1, :]
        whole = pltpu.roll(jnp.broadcast_to(line, (L, L)), 0, 1, stride=1, stride_axis=0)
        high = whole.astype(BF16)
        low = (whole - high.astype(F32)).astype(BF16)
        for i, part in ((0, high), (1, low)):
            now = part * upper
            band[c, r, L:, L * i : L * i + L] = now
            band[c, r, :L, L * i : L * i + L] = part - now


def convolve(c, pt, st, band, mixed, back):
    for r in range(GROUPS):
        rows = slice(CH * r, CH * r + CH)
        left = [x[c, part, rows, L * b : L * b + 2 * L] for x in (pt, st) for part in (0, 1) for b in (0, 1)]
        got = dot(jnp.concatenate(left, axis=0), band[c, r], ((1,), (0,)))
        for i, out in enumerate((mixed, back)):
            for b in (0, 1):
                high, low = CH * (4 * i + b), CH * (4 * i + 2 + b)
                out[rows, L * b : L * b + L] = (
                    got[high : high + CH, :L] + got[high : high + CH, L:] + got[low : low + CH, :L]
                )


def finish(c, k, v, g, mixed, back, gq, gk, gv):
    forward = jnp.transpose(mixed[...])
    backward = flip(jnp.transpose(back[...]))
    gq[:, lanes(c)] = (g[:, lanes(c)].astype(F32) * forward).astype(BF16)
    gk[:, lanes(c)] = (backward * v[:, lanes(c)].astype(F32)).astype(BF16)
    gv[:, lanes(c)] = (backward * k[:, lanes(c)].astype(F32)).astype(BF16)


def kernel(
    ny, nx, rows_here,
    k_hbm, v_hbm, q_hbm, g_hbm, taps_in, decay_in,
    gq, gk, gv, gf,
    k, v, q, g, kv_halo, qg_halo, pt, st, band, diag, folded, taps, lag, mixed, back,
    gather, partial, reduced, all_taps,
    in_sem, kv_send, kv_recv, qg_send, qg_recv, send, recv, ready,
):
    n = ny * nx * 2
    me = lax.axis_index("ctx")
    chip, core = me // 2, me % 2
    nxt, prv = (me + 1) % n, (me + n - 1) % n
    tokens = 2 * L
    half = CHUNKS * LANES // 2
    groups = taps_in.shape[1]

    def hops(dy, dx):
        return min(dy, ny - dy) + min(dx, nx - dx)

    steps = [(dy, dx) for dy in range(ny) for dx in range(nx) if dy or dx]
    steps.sort(key=lambda step: -hops(*step))
    chips = [((chip // nx + dy) % ny) * nx + (chip % nx + dx) % nx for dy, dx in steps]
    everyone = [device for there in chips for device in (2 * there, 2 * there + 1)] + [me + 1 - 2 * core]

    loads = [
        pltpu.make_async_copy(src, dst, in_sem.at[i])
        for i, (src, dst) in enumerate(((k_hbm, k), (v_hbm, v), (g_hbm, g), (q_hbm, q)))
    ]

    def halo_copies(piece, lead, sources, first, dst, sends, recvs, there):
        columns = slice(lead + piece * LANES, lead + (piece + 1) * LANES) if piece < 2 else slice(half - lead, 2 * half - lead)
        return [
            pltpu.make_async_remote_copy(
                src_ref=src.at[first : first + L, columns], dst_ref=dst.at[i, :, columns],
                send_sem=sends.at[piece, i], recv_sem=recvs.at[piece, i],
                device_id={"ctx": there}, device_id_type=MESH,
            )
            for i, src in enumerate(sources)
        ]

    def kv_copies(piece):
        return halo_copies(piece, 0, (k, v), tokens - L, kv_halo, kv_send, kv_recv, nxt)

    def qg_copies(piece):
        return halo_copies(piece, half, (g, q), 0, qg_halo, qg_send, qg_recv, prv)

    def send_to(which, src, dst, there):
        return pltpu.make_async_remote_copy(
            src_ref=src, dst_ref=dst, send_sem=send.at[which], recv_sem=recv.at[which],
            device_id={"ctx": there}, device_id_type=MESH,
        )

    def bytes_of(which, slots):
        return send_to(which, slots, slots, nxt)

    for copy in loads:
        copy.start()

    def along_y(dy):
        return 2 * (((chip // nx + ny + dy) % ny) * nx + chip % nx) + core

    row = [2 * ((chip // nx) * nx + (chip % nx + dx) % nx) for dx in range(nx)]
    def around(*distances):
        return sorted({d % ny for r in distances for d in (r, -r)} - {0})

    near = [nxt, prv, me + 1 - 2 * core] + [along_y(d) for d in around(1, 2)]
    row_mates = [me + 1 - 2 * core] + [there + c for there in row[1:] for c in (0, 1)]
    near += row_mates[1:]
    barrier = pltpu.get_barrier_semaphore()
    for there in near:
        pl.semaphore_signal(barrier, inc=1, device_id={"ctx": there}, device_id_type=MESH)

    mine = jnp.concatenate([taps_in[...], jnp.zeros((rows_here, L - groups), F32)], axis=1)
    place = me % (2 * nx)
    gather[pl.ds(chip // nx, 1), pl.ds(place, 1)] = mine[None, None]

    for copy in loads:
        copy.wait()
    pl.semaphore_wait(barrier, len(near))
    def tell(which, *distances):
        for d in around(*distances):
            pl.semaphore_signal(ready.at[which], inc=1, device_id={"ctx": along_y(d)}, device_id_type=MESH)

    my_row = gather.at[chip // nx]
    for there in row_mates:
        send_to(0, my_row.at[place], my_row.at[place], there).start()
    for piece in range(3):
        for copy in kv_copies(piece) + qg_copies(piece):
            copy.start()
    tell(0, 1, 2)

    def prepare_step(c, carry):
        prepare(c, k, v, g, q, pt, st)
        return carry

    lax.fori_loop(0, CHUNKS, prepare_step, 0)
    pl.semaphore_wait(ready.at[0], len(around(1, 2)))
    tell(1, 2)

    def inner_step(c, carry):
        lag_inner(c, pt, st, diag)
        return carry

    lax.fori_loop(0, CHUNKS, inner_step, 0)
    bytes_of(0, my_row.at[: 2 * nx - 1]).wait_recv()
    for d in sorted(range(1, ny), key=lambda d: -hops(d, 0)):
        send_to(1, my_row, my_row, along_y(d)).start()

    def kv_arrived(piece, chunks):
        for copy in kv_copies(piece):
            copy.wait_recv()
        for c in chunks:
            prepare_halo(c, kv_halo, pt, False, me > 0)

    def qg_arrived(piece, chunks):
        for copy in qg_copies(piece):
            copy.wait_recv()
        for c in chunks:
            prepare_halo(c, qg_halo, st, True, me < n - 1)

    def cross_step(i, carry):
        c = (i + 2 - 2 * core) % CHUNKS
        h = c // 2
        for piece in range(2):

            @pl.when(c == piece)
            def _():
                kv_arrived(piece, [piece])

            @pl.when(c == 2 + piece)
            def _():
                qg_arrived(piece, [2 + piece])

        lag_cross(c, pt, st, 2 * h, 2 - 2 * h, diag, folded, lag)
        return carry

    lax.fori_loop(0, CHUNKS, cross_step, 0)

    per_lag = jnp.transpose(
        jnp.concatenate([lag[c] for c in range(CHUNKS)] + [jnp.zeros((L - CHUNKS * GROUPS, L), F32)], axis=0)
    )
    for i in range(n):
        partial[i] = per_lag[L - rows_here * (i + 1) : L - rows_here * i]
    reduced[pl.ds(me, 1)] = partial[pl.ds(me, 1)]
    pl.semaphore_wait(ready.at[1], len(around(2)))
    for there in everyone:
        send_to(2, partial.at[there], reduced.at[me], there).start()

    bytes_of(1, gather.at[: ny - 1]).wait_recv()
    for i in range(n):
        all_taps[rows_here * i : rows_here * (i + 1), :] = gather[i // (2 * nx), i % (2 * nx)]
    decay = jnp.concatenate([decay_in[...], jnp.zeros((1, L - groups), F32)], axis=1)
    step = lax.broadcasted_iota(jnp.int32, (L, L), 0).astype(F32)
    turned = jnp.transpose(all_taps[...] * jnp.exp(-decay * step))
    for c in range(CHUNKS):
        taps[c] = turned[GROUPS * c : GROUPS * c + GROUPS]

    def output_step(c, carry):
        toeplitz(c, taps, band)
        convolve(c, pt, st, band, mixed, back)
        finish(c, k, v, g, mixed, back, gq, gk, gv)
        return carry

    def output_half(i):
        h = (i + core) % 2

        @pl.when(h == 0)
        def _():
            qg_arrived(2, [0, 1])

        @pl.when(h == 1)
        def _():
            kv_arrived(2, [2, 3])

        lax.fori_loop(2 * h, 2 * h + 2, output_step, 0)

    output_half(0)
    output_half(1)

    bytes_of(2, reduced.at[: n - 1]).wait_recv()
    total = jnp.sum(reduced[...], axis=0)
    total = jnp.concatenate([total[i : i + 1] for i in reversed(range(rows_here))], axis=0)
    lag_index = (me * rows_here + lax.broadcasted_iota(jnp.int32, (rows_here, L), 0)).astype(F32)
    gf[...] = (total * jnp.exp(-decay * lag_index) / float(tokens * n))[:, :groups]

    for piece in range(3):
        for copy in kv_copies(piece) + qg_copies(piece):
            copy.wait_send()
    bytes_of(0, my_row.at[: 2 * nx - 1]).wait_send()
    bytes_of(1, gather.at[: ny - 1]).wait_send()
    bytes_of(2, reduced.at[: n - 1]).wait_send()


def write_out(*refs):
    count = len(refs) // 2
    sems = refs[-1]
    copies = [pltpu.make_async_copy(refs[i], refs[count + i], sems.at[i]) for i in range(count)]
    for copy in copies:
        copy.start()
    for copy in copies:
        copy.wait()


def on_device(ny, nx, query_act, key_act, value_act, grad_gated, filter_taps, decay_rate):
    tokens, channels = query_act.shape
    rows_here, groups = filter_taps.shape
    whole = jax.ShapeDtypeStruct((tokens, channels), BF16)
    shapes = (whole, whole, whole, jax.ShapeDtypeStruct((rows_here, groups), F32))
    vmem = pl.BlockSpec(memory_space=pltpu.VMEM)
    hbm = pl.BlockSpec(memory_space=pl.ANY)
    dma = pltpu.SemaphoreType.DMA
    inner = pltpu.VMEM((tokens, channels), BF16)
    halo = pltpu.VMEM((2, L, channels), BF16)
    wide = pltpu.VMEM((CHUNKS, 2, LANES, 3 * L), BF16)
    by_device = pltpu.VMEM((2 * ny * nx, rows_here, L), F32)
    results = pl.pallas_call(
        functools.partial(kernel, ny, nx, rows_here),
        out_shape=shapes,
        in_specs=[hbm] * 4 + [vmem] * 2,
        out_specs=(vmem,) * 4,
        scratch_shapes=[
            inner, inner, inner, inner, halo, halo, wide, wide,
            pltpu.VMEM((CHUNKS, GROUPS, 2 * L, 2 * L), BF16),
            pltpu.VMEM((CHUNKS, GROUPS, L, L), F32),
            pltpu.VMEM((8 * GROUPS, L), F32),
            pltpu.VMEM((CHUNKS, GROUPS, L), F32),
            pltpu.VMEM((CHUNKS, GROUPS, L), F32),
            pltpu.VMEM((LANES, tokens), F32),
            pltpu.VMEM((LANES, tokens), F32),
            pltpu.VMEM((ny, 2 * nx, rows_here, L), F32),
            by_device, by_device,
            pltpu.VMEM((L, L), F32),
            dma((6,)), dma((3, 2)), dma((3, 2)), dma((3, 2)), dma((3, 2)), dma((3,)), dma((3,)), pltpu.SemaphoreType.REGULAR((2,)),
        ],
        compiler_params=pltpu.CompilerParams(
            collective_id=0, has_side_effects=True, vmem_limit_bytes=VMEM_LIMIT
        ),
    )(key_act, value_act, query_act, grad_gated, filter_taps, decay_rate.reshape(1, groups))
    return pl.pallas_call(
        write_out,
        out_shape=shapes,
        in_specs=[vmem] * 4,
        out_specs=(hbm,) * 4,
        scratch_shapes=[dma((4,))],
        compiler_params=pltpu.CompilerParams(vmem_limit_bytes=4 * 1024 * 1024),
    )(*results)


def solution(mesh):
    chips = mesh.shape["ctx"] // 2
    nx = 4 if chips >= 32 else 2
    return jax.shard_map(
        functools.partial(on_device, chips // nx, nx),
        mesh=mesh,
        in_specs=(P("ctx", "tp"),) * 5 + (P("tp"),),
        out_specs=(P("ctx", "tp"),) * 4,
        check_vma=False,
    )
```

time: 28 us -> 23 us (0.82)
  Pallas kernels: 26.5 us -> 21.5 us
    pallas_call x1, Pallas kernels: 25.6 us -> 20.6 us  [on_device(): pl.pallas_call(functools.partial(kernel, ny, nx, rows_here), out_shape=sh...]
where the time goes in v3:
time: 23 us; the launch traced here: 22.8 us
  Pallas kernels  21.5 us (93%)
  local copies, waits for them, and re-layouts  0.68 us (3%)
  between operations  0.66 us (3%)
    pallas_call x1, Pallas kernels, on_device(): pl.pallas_call(functools.partial(kernel, ny, nx, rows_here), out_shape=sh...  20.6 us
    pallas_call x1, Pallas kernels, on_device(): pl.pallas_call(write_out, out_shape=shapes, in_specs=[vmem] * 4, out_spec...  0.91 us
    unnamed x4, local copies, waits for them, and re-layouts  0.68 us

profile of v3, /device:TPU:1, one launch (start us, length us, event | category | flops | bytes accessed | tf_op | source)
XLA Modules:
  0.0 22.8 jit_solution(18266136111124047900)
XLA Ops:
  0.6 0.0 copy-start.1
  0.6 0.0 copy-start
  0.7 0.6 %copy-done.1 = f32[32]{0:T(128)S(1)} copy-done((f32[32]{0:T(128)S(1)}, f32[32]{0:T(128)}, u32[]{:S(2)}) %copy-start.1) | copy-done | bytes 152
  1.3 0.0 copy-done
  1.3 20.6 %shard_map.93 = (bf16[256,512]{1,0:T(8,128)(2,1)S(1)}, bf16[256,512]{1,0:T(8,128)(2,1)S(1)}, bf16[256,512]{1,0:T(8,128)(2,1)S(1)}, f32[2,32]{1,0:T(2,128)S(1)}) custom-call(bf16[256,512]{1,0:T(8,128)(2,1)} %k_hbm.1, bf16[256,512]{1,0:T(8,128)(2,1)} %v_hbm.1, bf16[256,512]{1,0:T(8,128)(2,1)} %q_hbm.1, bf16[256,512]{1,0:T(8,128)(2,1)} %g_hbm.1, ...), custom_call_target="tpu_custom_call" | custom-call | tf_op jit(solution)/shard_map/pallas_call | solution.py:355
  21.9 0.9 %shard_map.94 = (bf16[256,512]{1,0:T(8,128)(2,1)}, bf16[256,512]{1,0:T(8,128)(2,1)}, bf16[256,512]{1,0:T(8,128)(2,1)}, f32[2,32]{1,0:T(2,128)}) custom-call(bf16[256,512]{1,0:T(8,128)(2,1)S(1)} %get-tuple-element.8.refs_0_, bf16[256,512]{1,0:T(8,128)(2,1)S(1)} %get-tuple-element.9.refs_1_, bf16[256,512]{1,0:T(8,128)(2,1)S(1)} %get-tuple-element.10.refs_2_, ...), custom_call_target="tpu_custom_call" | custom-call | tf_op jit(solution)/shard_map/pallas_call | solution.py:378
Async XLA Ops:
  0.6 0.7 %copy-start.1 = (f32[32]{0:T(128)S(1)}, f32[32]{0:T(128)}, u32[]{:S(2)}) copy-start(f32[32]{0:T(128)} %param.11) | copy-start | bytes 388
  0.6 0.7 %copy-start = (f32[2,32]{1,0:T(2,128)S(1)}, f32[2,32]{1,0:T(2,128)}, u32[]{:S(2)}) copy-start(f32[2,32]{1,0:T(2,128)} %taps_in.1) | copy-start | bytes 772

commit v4 on v3

--- a/solution.py
+++ b/solution.py
@@ -12,7 +12,7 @@
 LANES = 128
 CHUNKS = 4
 GROUPS = LANES // CH
-VMEM_LIMIT = 53 * 1024 * 1024
+VMEM_LIMIT = 32 * 1024 * 1024
 MESH = pl.DeviceIdType.MESH
 F32, BF16 = jnp.float32, jnp.bfloat16
 
@@ -139,10 +139,10 @@
 
 def kernel(
     ny, nx, rows_here,
-    k_hbm, v_hbm, q_hbm, g_hbm, taps_in, decay_in,
+    k_hbm, v_hbm, q_hbm, g_hbm, taps_hbm, decay_hbm,
     gq, gk, gv, gf,
     k, v, q, g, kv_halo, qg_halo, pt, st, band, diag, folded, taps, lag, mixed, back,
-    gather, partial, reduced, all_taps,
+    taps_in, decay_in, gather, partial, reduced, all_taps,
     in_sem, kv_send, kv_recv, qg_send, qg_recv, send, recv, ready,
 ):
     n = ny * nx * 2
@@ -151,7 +151,7 @@
     nxt, prv = (me + 1) % n, (me + n - 1) % n
     tokens = 2 * L
     half = CHUNKS * LANES // 2
-    groups = taps_in.shape[1]
+    groups = taps_hbm.shape[1]
 
     def hops(dy, dx):
         return min(dy, ny - dy) + min(dx, nx - dx)
@@ -192,7 +192,11 @@
     def bytes_of(which, slots):
         return send_to(which, slots, slots, nxt)
 
-    for copy in loads:
+    small = [
+        pltpu.make_async_copy(taps_hbm, taps_in, in_sem.at[4]),
+        pltpu.make_async_copy(decay_hbm, decay_in, in_sem.at[5]),
+    ]
+    for copy in small + loads:
         copy.start()
 
     def along_y(dy):
@@ -209,12 +213,20 @@
     for there in near:
         pl.semaphore_signal(barrier, inc=1, device_id={"ctx": there}, device_id_type=MESH)
 
+    for copy in small:
+        copy.wait()
     mine = jnp.concatenate([taps_in[...], jnp.zeros((rows_here, L - groups), F32)], axis=1)
     place = me % (2 * nx)
     gather[pl.ds(chip // nx, 1), pl.ds(place, 1)] = mine[None, None]
 
     for copy in loads:
         copy.wait()
+    def prepare_step(c, carry):
+        prepare(c, k, v, g, q, pt, st)
+        return carry
+
+    lax.fori_loop(0, CHUNKS, prepare_step, 0)
+
     pl.semaphore_wait(barrier, len(near))
     def tell(which, *distances):
         for d in around(*distances):
@@ -223,27 +235,20 @@
     my_row = gather.at[chip // nx]
     for there in row_mates:
         send_to(0, my_row.at[place], my_row.at[place], there).start()
-    for piece in range(3):
+    for piece in range(2):
         for copy in kv_copies(piece) + qg_copies(piece):
             copy.start()
     tell(0, 1, 2)
-
-    def prepare_step(c, carry):
-        prepare(c, k, v, g, q, pt, st)
-        return carry
-
-    lax.fori_loop(0, CHUNKS, prepare_step, 0)
-    pl.semaphore_wait(ready.at[0], len(around(1, 2)))
-    tell(1, 2)
+    for copy in kv_copies(2) + qg_copies(2):
+        copy.start()
 
     def inner_step(c, carry):
         lag_inner(c, pt, st, diag)
         return carry
 
     lax.fori_loop(0, CHUNKS, inner_step, 0)
-    bytes_of(0, my_row.at[: 2 * nx - 1]).wait_recv()
-    for d in sorted(range(1, ny), key=lambda d: -hops(d, 0)):
-        send_to(1, my_row, my_row, along_y(d)).start()
+    pl.semaphore_wait(ready.at[0], len(around(1, 2)))
+    tell(1, 2)
 
     def kv_arrived(piece, chunks):
         for copy in kv_copies(piece):
@@ -273,7 +278,13 @@
         lag_cross(c, pt, st, 2 * h, 2 - 2 * h, diag, folded, lag)
         return carry
 
-    lax.fori_loop(0, CHUNKS, cross_step, 0)
+    lax.fori_loop(0, 2, cross_step, 0)
+
+    bytes_of(0, my_row.at[: 2 * nx - 1]).wait_recv()
+    for d in sorted(range(1, ny), key=lambda d: -hops(d, 0)):
+        send_to(1, my_row, my_row, along_y(d)).start()
+
+    lax.fori_loop(2, CHUNKS, cross_step, 0)
 
     per_lag = jnp.transpose(
         jnp.concatenate([lag[c] for c in range(CHUNKS)] + [jnp.zeros((L - CHUNKS * GROUPS, L), F32)], axis=0)
@@ -352,10 +363,12 @@
     halo = pltpu.VMEM((2, L, channels), BF16)
     wide = pltpu.VMEM((CHUNKS, 2, LANES, 3 * L), BF16)
     by_device = pltpu.VMEM((2 * ny * nx, rows_here, L), F32)
+    operands = (key_act, value_act, query_act, grad_gated, filter_taps, decay_rate.reshape(1, groups))
+    operands = [pltpu.with_memory_space_constraint(x, pltpu.HBM) for x in operands]
     results = pl.pallas_call(
         functools.partial(kernel, ny, nx, rows_here),
         out_shape=shapes,
-        in_specs=[hbm] * 4 + [vmem] * 2,
+        in_specs=[hbm] * 6,
         out_specs=(vmem,) * 4,
         scratch_shapes=[
             inner, inner, inner, inner, halo, halo, wide, wide,
@@ -366,6 +379,8 @@
             pltpu.VMEM((CHUNKS, GROUPS, L), F32),
             pltpu.VMEM((LANES, tokens), F32),
             pltpu.VMEM((LANES, tokens), F32),
+            pltpu.VMEM((rows_here, groups), F32),
+            pltpu.VMEM((1, groups), F32),
             pltpu.VMEM((ny, 2 * nx, rows_here, L), F32),
             by_device, by_device,
             pltpu.VMEM((L, L), F32),
@@ -374,7 +389,7 @@
         compiler_params=pltpu.CompilerParams(
             collective_id=0, has_side_effects=True, vmem_limit_bytes=VMEM_LIMIT
         ),
-    )(key_act, value_act, query_act, grad_gated, filter_taps, decay_rate.reshape(1, groups))
+    )(*operands)
     return pl.pallas_call(
         write_out,
         out_shape=shapes,

time: 23 us -> 21.9 us (0.952)
  local copies, waits for them, and re-layouts: 0.68 us -> 0 us
  Pallas kernels: 21.5 us -> 21.1 us
    unnamed x4 -> x0, local copies, waits for them, and re-layouts: 0.68 us -> none
    pallas_call x1, Pallas kernels: 20.6 us -> 20.2 us  [on_device(): pl.pallas_call(functools.partial(kernel, ny, nx, rows_here), out_shape=sh...]
where the time goes in v4:
time: 21.9 us; the launch traced here: 21.7 us
  Pallas kernels  21.1 us (96%)
  between operations  0.64 us (3%)
    pallas_call x1, Pallas kernels, on_device(): pl.pallas_call(functools.partial(kernel, ny, nx, rows_here), out_shape=sh...  20.2 us
    pallas_call x1, Pallas kernels, on_device(): pl.pallas_call(write_out, out_shape=shapes, in_specs=[vmem] * 4, out_spec...  0.91 us

profile of v4, /device:TPU:1, one launch (start us, length us, event | category | flops | bytes accessed | tf_op | source)
XLA Modules:
  0.0 21.7 jit_solution(13984122198083803730)
XLA Ops:
  0.6 20.2 %shard_map.93 = (bf16[256,512]{1,0:T(8,128)(2,1)S(1)}, bf16[256,512]{1,0:T(8,128)(2,1)S(1)}, bf16[256,512]{1,0:T(8,128)(2,1)S(1)}, f32[2,32]{1,0:T(2,128)S(1)}) custom-call(bf16[256,512]{1,0:T(8,128)(2,1)} %k_hbm.1, bf16[256,512]{1,0:T(8,128)(2,1)} %v_hbm.1, bf16[256,512]{1,0:T(8,128)(2,1)} %q_hbm.1, bf16[256,512]{1,0:T(8,128)(2,1)} %g_hbm.1, ...), custom_call_target="tpu_custom_call" | custom-call | tf_op jit(solution)/shard_map/pallas_call | solution.py:368
  20.8 0.9 %shard_map.94 = (bf16[256,512]{1,0:T(8,128)(2,1)}, bf16[256,512]{1,0:T(8,128)(2,1)}, bf16[256,512]{1,0:T(8,128)(2,1)}, f32[2,32]{1,0:T(2,128)}) custom-call(bf16[256,512]{1,0:T(8,128)(2,1)S(1)} %get-tuple-element.8.refs_0_, bf16[256,512]{1,0:T(8,128)(2,1)S(1)} %get-tuple-element.9.refs_1_, bf16[256,512]{1,0:T(8,128)(2,1)S(1)} %get-tuple-element.10.refs_2_, ...), custom_call_target="tpu_custom_call" | custom-call | tf_op jit(solution)/shard_map/pallas_call | solution.py:393

commit v5 on v4

--- a/solution.py
+++ b/solution.py
@@ -52,29 +52,40 @@
     out[c, 1, :, :L] = low * keep
 
 
-def lag_inner(c, pt, st, diag):
+def diagonals(whole):
+    return jnp.sum(pltpu.roll(whole, 0, 1, stride=1, stride_axis=0), axis=0, keepdims=True)
+
+
+def lag_pairs(c, r, pt, st, before, after):
+    rows = slice(CH * r, CH * r + CH)
+    none = jnp.zeros((CH, L), BF16)
+    p = [[pt[c, part, rows, L * b : L * b + L] for b in range(0 if before else 1, 3)] for part in (0, 1)]
+    s = [[st[c, part, rows, L * b : L * b + L] for b in range(0 if after else 1, 3)] for part in (0, 1)]
+    left = p[0] + p[1] + p[0]
+    right = []
+    for part in (0, 0, 1):
+        last = s[part][0] if after else none
+        if before:
+            right.append(jnp.concatenate([none, s[part][-1]], axis=1))
+        right.append(jnp.concatenate([s[part][-1], s[part][-2]], axis=1))
+        right.append(jnp.concatenate([s[part][-2], last], axis=1))
+    both = dot(jnp.concatenate(left, axis=0), jnp.concatenate(right, axis=0), ((0,), (0,)))
     row = lax.broadcasted_iota(jnp.int32, (L, L), 0)
     lane = lax.broadcasted_iota(jnp.int32, (L, L), 1)
-    upper = lane + row < L
-    none = jnp.zeros((CH, L), BF16)
+    return jnp.where(lane + row < L, both[:, :L], both[:, L:])
+
+
+def lag_inner(c, pt, st, diag):
     for r in range(GROUPS):
-        rows = slice(CH * r, CH * r + CH)
-        p = [[pt[c, part, rows, L * b : L * b + L] for b in (1, 2)] for part in (0, 1)]
-        s = [[st[c, part, rows, L * b : L * b + L] for b in (2, 1)] for part in (0, 1)]
-        left = jnp.concatenate([p[0][0], p[0][1], p[1][0], p[1][1], p[0][0], p[0][1]], axis=0)
-        right = jnp.concatenate(
-            [
-                jnp.concatenate([s[part][0], s[part][1]], axis=1) if b == 0 else jnp.concatenate([s[part][1], none], axis=1)
-                for part in (0, 0, 1)
-                for b in (0, 1)
-            ],
-            axis=0,
-        )
-        both = dot(left, right, ((0,), (0,)))
-        diag[c, r] = jnp.where(upper, both[:, :L], both[:, L:])
-
-
-def lag_cross(c, pt, st, pb, sb, diag, folded, lag):
+        diag[c % 2, r] = lag_pairs(c, r, pt, st, False, False)
+
+
+def lag_whole(c, pt, st, before, lag):
+    for r in range(GROUPS):
+        lag[c, r : r + 1, :] = diagonals(lag_pairs(c, r, pt, st, before, not before))
+
+
+def lag_cross(c, pt, st, pb, sb, diag, lag):
     row = lax.broadcasted_iota(jnp.int32, (L, L), 0)
     lane = lax.broadcasted_iota(jnp.int32, (L, L), 1)
     upper = lane + row < L
@@ -90,37 +101,26 @@
                 right.append(jnp.concatenate([s[j], none] if e == 0 else [none, s[j]], axis=1))
         both = dot(jnp.concatenate(left, axis=0), jnp.concatenate(right, axis=0), ((0,), (0,)))
         for e in range(2):
-            whole = diag[c, r + e] + jnp.where(upper, 0.0, both[:, L * e : L * e + L])
-            total = whole[:8]
-            for a in range(8, L, 8):
-                total = total + pltpu.roll(whole[a : a + 8], a, 1)
-            folded[8 * (r + e) : 8 * (r + e) + 8, :] = total
-    total = folded[pl.ds(0, GROUPS, stride=8), :]
-    for a in range(1, 8):
-        total = total + pltpu.roll(folded[pl.ds(a, GROUPS, stride=8), :], a, 1)
-    lag[c] = total
-
-
-def toeplitz(c, taps, band):
+            whole = diag[c % 2, r + e] + jnp.where(upper, 0.0, both[:, L * e : L * e + L])
+            lag[c, r + e : r + e + 1, :] = diagonals(whole)
+
+
+def filter_matrix(line, upper):
+    whole = pltpu.roll(jnp.broadcast_to(line, (L, L)), 0, 1, stride=1, stride_axis=0)
+    high = whole.astype(BF16)
+    low = (whole - high.astype(F32)).astype(BF16)
+    now = jnp.concatenate([high * upper, low * upper], axis=1)
+    return jnp.concatenate([jnp.concatenate([high, low], axis=1) - now, now], axis=0)
+
+
+def convolve(c, pt, st, taps, mixed, back):
     row = lax.broadcasted_iota(jnp.int32, (L, L), 0)
     lane = lax.broadcasted_iota(jnp.int32, (L, L), 1)
     upper = jnp.where(lane >= row, 1.0, 0.0).astype(BF16)
     for r in range(GROUPS):
-        line = taps[c, r : r + 1, :]
-        whole = pltpu.roll(jnp.broadcast_to(line, (L, L)), 0, 1, stride=1, stride_axis=0)
-        high = whole.astype(BF16)
-        low = (whole - high.astype(F32)).astype(BF16)
-        for i, part in ((0, high), (1, low)):
-            now = part * upper
-            band[c, r, L:, L * i : L * i + L] = now
-            band[c, r, :L, L * i : L * i + L] = part - now
-
-
-def convolve(c, pt, st, band, mixed, back):
-    for r in range(GROUPS):
         rows = slice(CH * r, CH * r + CH)
         left = [x[c, part, rows, L * b : L * b + 2 * L] for x in (pt, st) for part in (0, 1) for b in (0, 1)]
-        got = dot(jnp.concatenate(left, axis=0), band[c, r], ((1,), (0,)))
+        got = dot(jnp.concatenate(left, axis=0), filter_matrix(taps[c, r : r + 1, :], upper), ((1,), (0,)))
         for i, out in enumerate((mixed, back)):
             for b in (0, 1):
                 high, low = CH * (4 * i + b), CH * (4 * i + 2 + b)
@@ -141,7 +141,7 @@
     ny, nx, rows_here,
     k_hbm, v_hbm, q_hbm, g_hbm, taps_hbm, decay_hbm,
     gq, gk, gv, gf,
-    k, v, q, g, kv_halo, qg_halo, pt, st, band, diag, folded, taps, lag, mixed, back,
+    k, v, q, g, kv_halo, qg_halo, pt, st, diag, taps, lag, mixed, back,
     taps_in, decay_in, gather, partial, reduced, all_taps,
     in_sem, kv_send, kv_recv, qg_send, qg_recv, send, recv, ready,
 ):
@@ -192,6 +192,21 @@
     def bytes_of(which, slots):
         return send_to(which, slots, slots, nxt)
 
+    def along_y(dy):
+        return 2 * (((chip // nx + ny + dy) % ny) * nx + chip % nx) + core
+
+    row = [2 * ((chip // nx) * nx + (chip % nx + dx) % nx) for dx in range(nx)]
+    sorted_row = [row[dx] for dx in sorted(range(1, nx), key=lambda dx: -hops(0, dx))]
+
+    def around(*distances):
+        return sorted({d % ny for r in distances for d in (r, -r)} - {0})
+
+    row_mates = [there + c for there in sorted_row for c in (0, 1)] + [me + 1 - 2 * core]
+    near = [along_y(d) for d in around(2)] + row_mates[:2] + [nxt, prv] + [along_y(d) for d in around(1) if d not in around(2)] + row_mates[2:]
+    barrier = pltpu.get_barrier_semaphore()
+    for there in near:
+        pl.semaphore_signal(barrier, inc=1, device_id={"ctx": there}, device_id_type=MESH)
+
     small = [
         pltpu.make_async_copy(taps_hbm, taps_in, in_sem.at[4]),
         pltpu.make_async_copy(decay_hbm, decay_in, in_sem.at[5]),
@@ -199,20 +214,6 @@
     for copy in small + loads:
         copy.start()
 
-    def along_y(dy):
-        return 2 * (((chip // nx + ny + dy) % ny) * nx + chip % nx) + core
-
-    row = [2 * ((chip // nx) * nx + (chip % nx + dx) % nx) for dx in range(nx)]
-    def around(*distances):
-        return sorted({d % ny for r in distances for d in (r, -r)} - {0})
-
-    near = [nxt, prv, me + 1 - 2 * core] + [along_y(d) for d in around(1, 2)]
-    row_mates = [me + 1 - 2 * core] + [there + c for there in row[1:] for c in (0, 1)]
-    near += row_mates[1:]
-    barrier = pltpu.get_barrier_semaphore()
-    for there in near:
-        pl.semaphore_signal(barrier, inc=1, device_id={"ctx": there}, device_id_type=MESH)
-
     for copy in small:
         copy.wait()
     mine = jnp.concatenate([taps_in[...], jnp.zeros((rows_here, L - groups), F32)], axis=1)
@@ -232,21 +233,21 @@
         for d in around(*distances):
             pl.semaphore_signal(ready.at[which], inc=1, device_id={"ctx": along_y(d)}, device_id_type=MESH)
 
+    tell(0, 1, 2)
     my_row = gather.at[chip // nx]
     for there in row_mates:
         send_to(0, my_row.at[place], my_row.at[place], there).start()
     for piece in range(2):
         for copy in kv_copies(piece) + qg_copies(piece):
             copy.start()
-    tell(0, 1, 2)
-    for copy in kv_copies(2) + qg_copies(2):
-        copy.start()
 
     def inner_step(c, carry):
         lag_inner(c, pt, st, diag)
         return carry
 
-    lax.fori_loop(0, CHUNKS, inner_step, 0)
+    lax.fori_loop(2 * core, 2 * core + 2, inner_step, 0)
+    for copy in kv_copies(2) + qg_copies(2):
+        copy.start()
     pl.semaphore_wait(ready.at[0], len(around(1, 2)))
     tell(1, 2)
 
@@ -275,10 +276,31 @@
             def _():
                 qg_arrived(piece, [2 + piece])
 
-        lag_cross(c, pt, st, 2 * h, 2 - 2 * h, diag, folded, lag)
+        lag_cross(c, pt, st, 2 * h, 2 - 2 * h, diag, lag)
         return carry
 
-    lax.fori_loop(0, 2, cross_step, 0)
+    @pl.when(core == 0)
+    def _():
+        for piece in range(2):
+            qg_arrived(piece, [2 + piece])
+
+        def step(c, carry):
+            lag_whole(c, pt, st, False, lag)
+            return carry
+
+        lax.fori_loop(2, 4, step, 0)
+
+    @pl.when(core == 1)
+    def _():
+        for piece in range(2):
+            kv_arrived(piece, [piece])
+
+        def step(c, carry):
+            lag_whole(c, pt, st, True, lag)
+            return carry
+
+        lax.fori_loop(0, 2, step, 0)
+
 
     bytes_of(0, my_row.at[: 2 * nx - 1]).wait_recv()
     for d in sorted(range(1, ny), key=lambda d: -hops(d, 0)):
@@ -305,12 +327,6 @@
     for c in range(CHUNKS):
         taps[c] = turned[GROUPS * c : GROUPS * c + GROUPS]
 
-    def output_step(c, carry):
-        toeplitz(c, taps, band)
-        convolve(c, pt, st, band, mixed, back)
-        finish(c, k, v, g, mixed, back, gq, gk, gv)
-        return carry
-
     def output_half(i):
         h = (i + core) % 2
 
@@ -322,13 +338,18 @@
         def _():
             kv_arrived(2, [2, 3])
 
-        lax.fori_loop(2 * h, 2 * h + 2, output_step, 0)
+        for j in range(2):
+            convolve(2 * h + j, pt, st, taps, mixed.at[j], back.at[j])
+            finish(2 * h + j, k, v, g, mixed.at[j], back.at[j], gq, gk, gv)
 
     output_half(0)
     output_half(1)
 
     bytes_of(2, reduced.at[: n - 1]).wait_recv()
-    total = jnp.sum(reduced[...], axis=0)
+    parts = [jnp.sum(reduced[i : i + n // 8], axis=0) for i in range(0, n, n // 8)]
+    while len(parts) > 1:
+        parts = [parts[i] + parts[i + 1] for i in range(0, len(parts), 2)]
+    total = parts[0]
     total = jnp.concatenate([total[i : i + 1] for i in reversed(range(rows_here))], axis=0)
     lag_index = (me * rows_here + lax.broadcasted_iota(jnp.int32, (rows_here, L), 0)).astype(F32)
     gf[...] = (total * jnp.exp(-decay * lag_index) / float(tokens * n))[:, :groups]
@@ -372,13 +393,11 @@
         out_specs=(vmem,) * 4,
         scratch_shapes=[
             inner, inner, inner, inner, halo, halo, wide, wide,
-            pltpu.VMEM((CHUNKS, GROUPS, 2 * L, 2 * L), BF16),
-            pltpu.VMEM((CHUNKS, GROUPS, L, L), F32),
-            pltpu.VMEM((8 * GROUPS, L), F32),
+            pltpu.VMEM((2, GROUPS, L, L), F32),
             pltpu.VMEM((CHUNKS, GROUPS, L), F32),
             pltpu.VMEM((CHUNKS, GROUPS, L), F32),
-            pltpu.VMEM((LANES, tokens), F32),
-            pltpu.VMEM((LANES, tokens), F32),
+            pltpu.VMEM((2, LANES, tokens), F32),
+            pltpu.VMEM((2, LANES, tokens), F32),
             pltpu.VMEM((rows_here, groups), F32),
             pltpu.VMEM((1, groups), F32),
             pltpu.VMEM((ny, 2 * nx, rows_here, L), F32),

time: 21.9 us -> 21.7 us (level)
  no operation moved by 1% of the time
where the time goes in v5:
time: 21.7 us; the launch traced here: 21.6 us
  Pallas kernels  20.9 us (96%)
  between operations  0.64 us (3%)
    pallas_call x1, Pallas kernels, on_device(): pl.pallas_call(functools.partial(kernel, ny, nx, rows_here), out_shape=sh...  20 us
    pallas_call x1, Pallas kernels, on_device(): pl.pallas_call(write_out, out_shape=shapes, in_specs=[vmem] * 4, out_spec...  0.91 us

profile of v5, /device:TPU:1, one launch (start us, length us, event | category | flops | bytes accessed | tf_op | source)
XLA Modules:
  0.0 21.6 jit_solution(15220799749278782815)
XLA Ops:
  0.6 20.0 %shard_map.93 = (bf16[256,512]{1,0:T(8,128)(2,1)S(1)}, bf16[256,512]{1,0:T(8,128)(2,1)S(1)}, bf16[256,512]{1,0:T(8,128)(2,1)S(1)}, f32[2,32]{1,0:T(2,128)S(1)}) custom-call(bf16[256,512]{1,0:T(8,128)(2,1)} %k_hbm.1, bf16[256,512]{1,0:T(8,128)(2,1)} %v_hbm.1, bf16[256,512]{1,0:T(8,128)(2,1)} %q_hbm.1, bf16[256,512]{1,0:T(8,128)(2,1)} %g_hbm.1, ...), custom_call_target="tpu_custom_call" | custom-call | tf_op jit(solution)/shard_map/pallas_call | solution.py:389
  20.6 0.9 %shard_map.94 = (bf16[256,512]{1,0:T(8,128)(2,1)}, bf16[256,512]{1,0:T(8,128)(2,1)}, bf16[256,512]{1,0:T(8,128)(2,1)}, f32[2,32]{1,0:T(2,128)}) custom-call(bf16[256,512]{1,0:T(8,128)(2,1)S(1)} %get-tuple-element.8.refs_0_, bf16[256,512]{1,0:T(8,128)(2,1)S(1)} %get-tuple-element.9.refs_1_, bf16[256,512]{1,0:T(8,128)(2,1)S(1)} %get-tuple-element.10.refs_2_, ...), custom_call_target="tpu_custom_call" | custom-call | tf_op jit(solution)/shard_map/pallas_call | solution.py:412

commit v6 on v5

--- a/solution.py
+++ b/solution.py
@@ -220,14 +220,6 @@
     place = me % (2 * nx)
     gather[pl.ds(chip // nx, 1), pl.ds(place, 1)] = mine[None, None]
 
-    for copy in loads:
-        copy.wait()
-    def prepare_step(c, carry):
-        prepare(c, k, v, g, q, pt, st)
-        return carry
-
-    lax.fori_loop(0, CHUNKS, prepare_step, 0)
-
     pl.semaphore_wait(barrier, len(near))
     def tell(which, *distances):
         for d in around(*distances):
@@ -237,9 +229,17 @@
     my_row = gather.at[chip // nx]
     for there in row_mates:
         send_to(0, my_row.at[place], my_row.at[place], there).start()
+    for copy in loads:
+        copy.wait()
     for piece in range(2):
         for copy in kv_copies(piece) + qg_copies(piece):
             copy.start()
+    def prepare_step(c, carry):
+        prepare(c, k, v, g, q, pt, st)
+        return carry
+
+    lax.fori_loop(0, CHUNKS, prepare_step, 0)
+
 
     def inner_step(c, carry):
         lag_inner(c, pt, st, diag)

time: 21.7 us -> 21.7 us (level)
  no operation moved by 1% of the time
where the time goes in v6:
time: 21.7 us; the launch traced here: 21.6 us
  Pallas kernels  20.9 us (96%)
  between operations  0.64 us (3%)
    pallas_call x1, Pallas kernels, on_device(): pl.pallas_call(functools.partial(kernel, ny, nx, rows_here), out_shape=sh...  20 us
    pallas_call x1, Pallas kernels, on_device(): pl.pallas_call(write_out, out_shape=shapes, in_specs=[vmem] * 4, out_spec...  0.91 us

profile of v6, /device:TPU:1, one launch (start us, length us, event | category | flops | bytes accessed | tf_op | source)
XLA Modules:
  0.0 21.6 jit_solution(9465338061883635255)
XLA Ops:
  0.6 20.0 %shard_map.93 = (bf16[256,512]{1,0:T(8,128)(2,1)S(1)}, bf16[256,512]{1,0:T(8,128)(2,1)S(1)}, bf16[256,512]{1,0:T(8,128)(2,1)S(1)}, f32[2,32]{1,0:T(2,128)S(1)}) custom-call(bf16[256,512]{1,0:T(8,128)(2,1)} %k_hbm.1, bf16[256,512]{1,0:T(8,128)(2,1)} %v_hbm.1, bf16[256,512]{1,0:T(8,128)(2,1)} %q_hbm.1, bf16[256,512]{1,0:T(8,128)(2,1)} %g_hbm.1, ...), custom_call_target="tpu_custom_call" | custom-call | tf_op jit(solution)/shard_map/pallas_call | solution.py:389
  20.7 0.9 %shard_map.94 = (bf16[256,512]{1,0:T(8,128)(2,1)}, bf16[256,512]{1,0:T(8,128)(2,1)}, bf16[256,512]{1,0:T(8,128)(2,1)}, f32[2,32]{1,0:T(2,128)}) custom-call(bf16[256,512]{1,0:T(8,128)(2,1)S(1)} %get-tuple-element.8.refs_0_, bf16[256,512]{1,0:T(8,128)(2,1)S(1)} %get-tuple-element.9.refs_1_, bf16[256,512]{1,0:T(8,128)(2,1)S(1)} %get-tuple-element.10.refs_2_, ...), custom_call_target="tpu_custom_call" | custom-call | tf_op jit(solution)/shard_map/pallas_call | solution.py:412
